TPU v7x, 256 devices: a whole 4x4x8 slice. The times are simulated.
256 devices in a mesh: table: 32 (over x, y, core), group: 8 (over z).
Axes of the slice: x: 4, y: 4, z: 8, core: 2. Of those that a mesh axis runs over, the one named last changes fastest.
Arguments:
- table: bfloat16 [32768, 512], P('table'), may hold values from -6 to 6
- fetch_rows: int32 [256, 32, 8], P(('table', 'group')), may hold values from 0 to 1023, as said below
- item_slot: int32 [65536], P(('table', 'group')), may hold values from 0 to 255, as said below
- seq_lengths: int32 [256, 8], P(('table', 'group')), may hold values from 1 to 128, 256 in all within a row
- w_in: bfloat16 [512, 2048], replicated, may hold values from -0.25 to 0.25
- w_out: bfloat16 [512, 512], replicated, may hold values from -0.25 to 0.25
- out_cot: bfloat16 [65536, 512], P(('table', 'group')), may hold values from -6 to 6
Outputs:
- layer_out: bfloat16 [65536, 512], P(('table', 'group'))
- table_grad: bfloat16 [8, 32768, 512], P('group', 'table')
- w_in_grad: float32 [512, 2048], replicated
- w_out_grad: float32 [512, 512], replicated
Inputs may be any that keep to these rules, and one draw needn't show every extreme that they name: `fetch_rows`: the 8 entries of one shard's list for one owner are distinct rows of that owner's shard. `item_slot`: entry c of a shard's list for owner o is slot o * 8 + c. In each group, for one owner drawn from the seed, every shard names all 8 entries of its list for that owner.
All inputs are finite; a program needn't handle non-finite values.
Results may differ from a plain program's by a relative error of at most 0.019.
Values may be sent and summed in bfloat16 or wider, within the bound.
A program may use at most 64 MiB of HBM per device.

v0:
```python
import jax
import jax.numpy as jnp
from jax import lax
from jax.sharding import PartitionSpec as P

HEADS = 8


EPS = 1e-05


def normalize(values):
    row_mean = jnp.mean(values, axis=-1, keepdims=True)
    centred = values - row_mean
    spread = jnp.mean(centred * centred, axis=-1, keepdims=True)
    return centred * lax.rsqrt(spread + EPS)


def segment_ids(lengths, token_count):
    sequence_ends = jnp.cumsum(lengths)
    positions = jnp.arange(token_count, dtype=jnp.int32)
    return jnp.sum((positions[:, None] >= sequence_ends[None, :]).astype(jnp.int32), axis=1)


def hstu_layer(embedded, w_in, w_out, segment):
    token_count, width = embedded.shape
    head_dim = width // HEADS
    block_rows = min(512, token_count)
    inputs32 = embedded.astype(jnp.float32)
    normed = normalize(inputs32).astype(jnp.bfloat16)
    projected = jax.nn.silu(jnp.dot(normed, w_in, preferred_element_type=jnp.float32)).astype(
        jnp.bfloat16
    )
    gate_u = projected[:, :width]
    value_heads = projected[:, width : 2 * width].reshape(token_count, HEADS, head_dim)
    queries = projected[:, 2 * width : 3 * width].reshape(token_count, HEADS, head_dim)
    key_heads = projected[:, 3 * width :].reshape(token_count, HEADS, head_dim)
    score_scale = head_dim ** (-0.5)
    positions = jnp.arange(token_count, dtype=jnp.int32)
    scores = (
        jnp.einsum("qhd,khd->hqk", queries, key_heads, preferred_element_type=jnp.float32)
        * score_scale
    )
    allowed = (segment[0:block_rows, None] == segment[None, :block_rows]) & (
        positions[0:block_rows, None] >= positions[None, :block_rows]
    )
    weights = jnp.where(allowed[None], jax.nn.silu(scores), 0.0).astype(jnp.bfloat16)
    mixed_block = jnp.einsum(
        "hqk,khd->qhd", weights, value_heads, preferred_element_type=jnp.float32
    )
    pieces = [mixed_block.reshape(block_rows, width)]
    mixed = jnp.concatenate(pieces, axis=0)
    gated = (normalize(mixed) * gate_u.astype(jnp.float32)).astype(jnp.bfloat16)
    return (inputs32 + jnp.dot(gated, w_out, preferred_element_type=jnp.float32)).astype(
        jnp.bfloat16
    )


def indicator_sum(indices, values, count):
    selector = (indices[:, None] == jnp.arange(count, dtype=jnp.int32)[None, :]).astype(
        jnp.bfloat16
    )
    return lax.dot_general(
        selector, values, (((0,), (0,)), ((), ())), preferred_element_type=jnp.float32
    )


def body(table, fetch_rows, item_slot, seq_lengths, w_in, w_out, out_cot):
    owners = lax.axis_size("table")
    width = table.shape[1]
    slot_total = fetch_rows.shape[1] * fetch_rows.shape[2]
    requested = lax.all_to_all(fetch_rows, "table", split_axis=1, concat_axis=0, tiled=True)
    found = jnp.take(table, requested, axis=0)
    delivered = lax.all_to_all(found, "table", split_axis=0, concat_axis=1, tiled=True)
    delivered, requested = (delivered, requested)
    gathered = delivered.reshape(slot_total, width)
    embedded = jnp.take(gathered, item_slot, axis=0)
    segment = segment_ids(seq_lengths[0], item_slot.shape[0])

    def layer(emb_rows, weight_in, weight_out):
        return hstu_layer(emb_rows, weight_in, weight_out, segment)

    layer_out, backward = jax.vjp(layer, embedded, w_in, w_out)
    d_embedded, grad_in, grad_out = backward(out_cot)
    slot_grad = indicator_sum(item_slot, d_embedded, slot_total).astype(jnp.bfloat16)
    arrived = lax.all_to_all(
        slot_grad.reshape(owners, slot_total // owners, width),
        "table",
        split_axis=0,
        concat_axis=0,
        tiled=True,
    )
    owner_sum = indicator_sum(requested.reshape(-1), arrived.reshape(-1, width), table.shape[0])
    table_grad = owner_sum.astype(jnp.bfloat16)[None]
    token_total = item_slot.shape[0] * owners * lax.axis_size("group")
    grad_scale = float(token_total) ** (-0.5)
    sum_in, sum_out = lax.psum(
        (grad_in.astype(jnp.float32), grad_out.astype(jnp.float32)), ("table", "group")
    )
    return (layer_out, table_grad, sum_in * grad_scale, sum_out * grad_scale)


def solution(mesh):
    placed = (
        P("table", None),
        P(("table", "group"), None, None),
        P(("table", "group")),
        P(("table", "group"), None),
        P(),
        P(),
        P(("table", "group"), None),
    )
    return jax.shard_map(
        body,
        mesh=mesh,
        in_specs=placed,
        out_specs=(P(("table", "group"), None), P("group", "table", None), P(), P()),
        check_vma=False,
    )
```

profile of v0, /device:TPU:1, one launch (start us, length us, event | category | flops | bytes accessed | tf_op | source)
XLA Modules:
  0.0 352.9 jit_solution(10762458909239708354)
XLA Ops:
  7.2 1.5 copy.44
  8.7 8.6 %all-to-all-start = ((s32[1,32,8]{2,0,1:T(1,128)}), s32[1,32,8]{2,0,1:T(1,128)S(1)}, u32[]{:S(2)}, u32[]{:S(2)}) async-start(s32[1,32,8]{2,0,1:T(1,128)} %copy.44), calls=%async_computation | async-start | bytes 32768 | tf_op jit(solution)/shard_map/all_to_all | solution.py:72
  17.3 0.7 compare_and_fusion.1
  18.0 0.7 compare_select_fusion.2
  18.7 0.8 reduce-window.8
  19.6 4.6 %all-to-all-done = s32[1,32,8]{2,0,1:T(1,128)S(1)} async-done(((s32[1,32,8]{2,0,1:T(1,128)}), s32[1,32,8]{2,0,1:T(1,128)S(1)}, u32[]{:S(2)}, u32[]{:S(2)}) %all-to-all-start) | async-done | bytes 1056 | tf_op jit(solution)/shard_map/all_to_all | solution.py:72
  24.3 2.6 gather_fusion
  26.9 0.8 bitcast_select_fusion
  27.7 4.2 %all-to-all-start.1 = ((bf16[32,1,8,512]{3,2,1,0:T(8,128)(2,1)}), bf16[32,1,8,512]{3,2,1,0:T(8,128)(2,1)S(1)}, u32[]{:S(2)}, u32[]{:S(2)}) async-start(bf16[32,1,8,512]{3,2,1,0:T(8,128)(2,1)} %bitcast_select_fusion), calls=%async_computation.1 | async-start | bytes 524288 | tf_op jit(solution)/shard_map/all_to_all | solution.py:74
  32.0 8.9 %all-to-all-done.1 = bf16[32,1,8,512]{3,2,1,0:T(8,128)(2,1)S(1)} async-done(((bf16[32,1,8,512]{3,2,1,0:T(8,128)(2,1)}), bf16[32,1,8,512]{3,2,1,0:T(8,128)(2,1)S(1)}, u32[]{:S(2)}, u32[]{:S(2)}) %all-to-all-start.1) | async-done | bytes 262176 | tf_op jit(solution)/shard_map/all_to_all | solution.py:74
  41.0 1.2 gather_fusion.1
  42.1 0.2 convert_reduce_fusion
  42.3 0.2 fusion.17
  42.6 2.1 multiply_convert_fusion
  44.7 1.0 copy-done.2
  45.8 0.1 copy.48
  45.9 0.1 copy.47
  46.1 0.1 copy.46
  46.2 2.1 select_convert_fusion
  48.3 0.5 fusion.37
  48.8 0.1 fusion.21
  48.9 0.4 copy-done.1
  49.3 0.2 copy.49
  49.5 1.6 multiply_reduce_fusion
  51.2 2.0 fusion.35
  53.1 0.1 broadcast_add_fusion
  53.3 0.1 copy.50
  53.4 2.2 fusion.38
  55.6 2.9 fusion.5
  58.6 1.1 fusion.39
  59.7 1.0 fusion.40
  60.7 0.8 copy.53
  61.6 1.8 copy.51
  63.4 0.8 copy.52
  64.2 1.3 fusion.7
  65.5 5.1 %fusion = f32[512,2048]{1,0:T(8,128)} fusion(f32[256]{0:T(256)S(1)} %fusion.27, f32[256]{0:T(256)S(1)} %broadcast_multiply_fusion.3, bf16[256,512]{1,0:T(8,128)(2,1)S(1)} %gather_fusion.1, pred[256]{0:T(512)(128)(4,1)S(1)} %compare_and_fusion.1, f32[256,2048]{1,0:T(8,128)} %get-tuple-element.16, bf16[256,512]{1,0:T(8,128)(2,1)S(1)} %copy-done.14, ...), kind=kOutput, calls=%fused_computation.5 | convolution fusion | flops 548536320 | bytes 7604480 | tf_op jit(solution)/shard_map/transpose(jvp())/dot_general | solution.py:31
  70.6 0.5 broadcast.218
  71.2 0.7 reduce.6
  72.0 3.3 fusion.19
  75.3 0.3 fusion.32
  75.6 1.3 fusion.11
  76.8 3.7 %all-to-all-start.2 = ((bf16[32,8,512]{2,1,0:T(8,128)(2,1)}), bf16[32,8,512]{2,1,0:T(8,128)(2,1)S(1)}, u32[]{:S(2)}, u32[]{:S(2)}) async-start(bf16[32,8,512]{2,1,0:T(8,128)(2,1)} %fusion.11), calls=%async_computation.2 | async-start | bytes 524288 | tf_op jit(solution)/shard_map/all_to_all | solution.py:86
  80.6 1.0 fusion.9
  81.6 8.1 %all-to-all-done.2 = bf16[32,8,512]{2,1,0:T(8,128)(2,1)S(1)} async-done(((bf16[32,8,512]{2,1,0:T(8,128)(2,1)}), bf16[32,8,512]{2,1,0:T(8,128)(2,1)S(1)}, u32[]{:S(2)}, u32[]{:S(2)}) %all-to-all-start.2) | async-done | bytes 262176 | tf_op jit(solution)/shard_map/all_to_all | solution.py:86
  89.7 1.5 fusion.6
  91.2 248.9 %all-reduce.7.cloned.1.call-done = (f32[512,2048]{1,0:T(8,128)}, f32[512,512]{1,0:T(8,128)}) async-done(((f32[512,2048]{1,0:T(8,128)}, f32[512,512]{1,0:T(8,128)}), (f32[512,2048]{1,0:T(8,128)}, f32[512,512]{1,0:T(8,128)})) %all-reduce.7.cloned.1.call-update) | async-done | bytes 5242896 | tf_op jit(solution)/shard_map/psum | solution.py:97
  340.1 4.9 %broadcast_multiply_fusion = f32[512,2048]{1,0:T(8,128)} fusion(f32[512,2048]{1,0:T(8,128)} %get-tuple-element.4), kind=kLoop, calls=%fused_computation.13 | loop fusion | flops 1048576 | bytes 8388608 | tf_op jit(solution)/shard_map/mul | solution.py:100
  345.0 1.1 broadcast_multiply_fusion.1
  (50 shorter events, 0.6 us)
Async XLA Ops:
  7.2 35.4 %copy-start = (bf16[512,2048]{1,0:T(8,128)(2,1)S(1)}, bf16[512,2048]{1,0:T(8,128)(2,1)}, u32[]{:S(2)}) copy-start(bf16[512,2048]{1,0:T(8,128)(2,1)} %param.11) | copy-start | bytes 6291460
  8.7 15.5 %all-to-all-start = ((s32[1,32,8]{2,0,1:T(1,128)}), s32[1,32,8]{2,0,1:T(1,128)S(1)}, u32[]{:S(2)}, u32[]{:S(2)}) async-start(s32[1,32,8]{2,0,1:T(1,128)} %copy.44), calls=%async_computation | async-start | bytes 32768 | tf_op jit(solution)/shard_map/all_to_all | solution.py:72
  27.7 13.3 %all-to-all-start.1 = ((bf16[32,1,8,512]{3,2,1,0:T(8,128)(2,1)}), bf16[32,1,8,512]{3,2,1,0:T(8,128)(2,1)S(1)}, u32[]{:S(2)}, u32[]{:S(2)}) async-start(bf16[32,1,8,512]{3,2,1,0:T(8,128)(2,1)} %bitcast_select_fusion), calls=%async_computation.1 | async-start | bytes 524288 | tf_op jit(solution)/shard_map/all_to_all | solution.py:74
  31.9 308.3 %all-reduce.7.cloned.1.call-start = ((), (), s32[]{:S(2)}) async-start(), calls=%async_computation.3 | async-start | bytes 10485760 | tf_op jit(solution)/shard_map/psum | solution.py:97
  44.7 1.0 copy-start.2
  45.9 2.4 copy-start.7
  46.1 2.3 copy-start.9
  46.2 2.1 copy-start.3
  48.3 1.0 copy-start.1
  51.1 4.5 %copy-start.4 = (bf16[256,512]{0,1:T(8,128)(2,1)S(1)}, bf16[256,512]{0,1:T(8,128)(2,1)}, u32[]{:S(2)}) copy-start(bf16[256,512]{0,1:T(8,128)(2,1)} %copy-done.3) | copy-start | bytes 786436
  55.6 2.9 copy-start.8
  55.6 4.1 %copy-start.10 = (bf16[256,512]{0,1:T(8,128)(2,1)S(1)}, bf16[256,512]{0,1:T(8,128)(2,1)}, u32[]{:S(2)}) copy-start(bf16[256,512]{0,1:T(8,128)(2,1)} %copy-done.9) | copy-start | bytes 786436
  58.5 2.2 copy-start.11
  58.5 5.7 %copy-start.6 = (bf16[256,512]{1,0:T(8,128)(2,1)S(1)}, bf16[256,512]{1,0:T(8,128)(2,1)}, u32[]{:S(2)}) copy-start(bf16[256,512]{1,0:T(8,128)(2,1)} %param.13) | copy-start | bytes 786436
  59.7 3.7 %copy-start.12 = (bf16[8,256,64]{1,2,0:T(8,128)(2,1)S(1)}, bf16[8,256,64]{1,2,0:T(8,128)(2,1)}, u32[]{:S(2)}) copy-start(bf16[8,256,64]{1,2,0:T(8,128)(2,1)} %fusion.39) | copy-start | bytes 786436
  61.6 4.0 %copy-start.14 = (bf16[256,512]{1,0:T(8,128)(2,1)S(1)}, bf16[256,512]{1,0:T(8,128)(2,1)}, u32[]{:S(2)}) copy-start(bf16[256,512]{1,0:T(8,128)(2,1)} %get-tuple-element.9) | copy-start | bytes 786436
  70.6 1.3 copy-start.15
  71.9 3.6 %copy-start.16 = (s32[256]{0:T(256)S(1)}, s32[256]{0:T(256)}, u32[]{:S(2)}) copy-start(s32[256]{0:T(256)} %param.9) | copy-start | bytes 3076
  75.2 5.3 %copy-start.13 = (bf16[512,512]{1,0:T(8,128)(2,1)S(1)}, bf16[512,512]{1,0:T(8,128)(2,1)}, u32[]{:S(2)}) copy-start(bf16[512,512]{1,0:T(8,128)(2,1)} %param.12) | copy-start | bytes 1572868
  76.8 12.9 %all-to-all-start.2 = ((bf16[32,8,512]{2,1,0:T(8,128)(2,1)}), bf16[32,8,512]{2,1,0:T(8,128)(2,1)S(1)}, u32[]{:S(2)}, u32[]{:S(2)}) async-start(bf16[32,8,512]{2,1,0:T(8,128)(2,1)} %fusion.11), calls=%async_computation.2 | async-start | bytes 524288 | tf_op jit(solution)/shard_map/all_to_all | solution.py:86
  340.1 4.9 %copy-start.5 = (f32[512,512]{1,0:T(8,128)S(1)}, f32[512,512]{1,0:T(8,128)}, u32[]{:S(2)}) copy-start(f32[512,512]{1,0:T(8,128)} %get-tuple-element.5) | copy-start | bytes 3145732
Sparse Core Ops, SparseCore 0:
  70.8 269.3 all-reduce.6
where the time goes:
time: 354 us; the launch traced here: 353 us
  waiting for transfers between devices  271 us (77%)
  matrix products  27 us (8%)
  starting transfers between devices  16.5 us (5%)
  between operations  14.3 us (4%)
  other arithmetic  12.8 us (4%)
  local copies, waits for them, and re-layouts  11.6 us (3%)
    psum x1, waiting for transfers between devices, body(): lax.psum((grad_in.astype(jnp.float32), grad_out.astype(jnp.float32)), ('t...  249 us
    dot_general x3, matrix products, hstu_layer(): jnp.dot(normed, w_in, preferred_element_type=jnp.float32)  10.5 us
    all_to_all x1, waiting for transfers between devices, body(): lax.all_to_all(found, 'table', split_axis=0, concat_axis=1, tiled=True)  8.93 us
    all_to_all x1, starting transfers between devices, body(): lax.all_to_all(fetch_rows, 'table', split_axis=1, concat_axis=0, tiled=True)  8.59 us
    all_to_all x1, waiting for transfers between devices, body(): lax.all_to_all(slot_grad.reshape(owners, slot_total // owners, width), 't...  8.14 us
  transfers between devices with their start and end apart: 4, of which 4 were waited for; matrix products, arithmetic and copies ran while one was open for 3% of the time, Pallas kernels for 0%

commit v1 on v0

v1 whole, which is shorter than its diff:
```python
import functools
import math

import jax
import jax.numpy as jnp
from jax import lax
from jax.experimental import pallas as pl
from jax.experimental.pallas import tpu as pltpu
from jax.sharding import PartitionSpec as P

HEADS = 8
EPS = 1e-05
MESH = pl.DeviceIdType.MESH
BF = jnp.bfloat16
F32 = jnp.float32

NN = (((1,), (0,)), ((), ()))
NT = (((1,), (1,)), ((), ()))
TN = (((0,), (0,)), ((), ()))


def mm(a, b, dims=NN):
    return lax.dot_general(a, b, dims, preferred_element_type=F32)


def rows_of(start, size):
    return pl.ds(pl.multiple_of(start, size), size)


def kernel(
    n, nz, count, cap, rows, tokens, width,
    fetch_ref, slot_ref, len_ref, table_hbm, win_hbm, wout_hbm, cot_hbm,
    out_ref, tg_ref, full_ref, fullo_ref,
    table_v, win_v, wout_v, cot_v,
    req_s, req_r, found, rows_r, sg_s, sg_r,
    emb, n32, normed, proj, dsil, dpre, weights, dfac, mixed, allowed,
    g, pr, h, r1, s1, r2, s2, r3, a2,
    ro1, ro2, so2, ro3,
    load_sem, send_sem, recv_sem,
):
    t = lax.axis_index("table")
    z = lax.axis_index("group")
    x = lax.div(t, 2 * n)
    y = lax.rem(lax.div(t, 2), n)
    c = lax.rem(t, 2)
    slots = count * cap
    half = width // 2
    R0 = width // 2
    R1 = R0 // n
    R2 = R1 // n
    CZ = 4 * width // nz

    def at(px, py, pc):
        return (px * n + py) * 2 + pc

    def plus(v, d, m):
        return lax.rem(v + d, m)

    offsets = [(dx, dy, dc) for dx in range(n) for dy in range(n) for dc in range(2)][1:]
    ahead = [at(plus(x, dx, n), plus(y, dy, n), plus(c, dc, 2)) for dx, dy, dc in offsets]
    behind = [at(plus(x, n - dx, n), plus(y, n - dy, n), plus(c, 2 - dc, 2)) for dx, dy, dc in offsets]
    zs = [plus(z, d, nz) for d in range(1, nz)]
    xs = [at(plus(x, d, n), y, c) for d in range(1, n)]
    ys = [at(x, plus(y, d, n), c) for d in range(1, n)]
    partner = at(x, y, 1 - c)

    loads = [
        pltpu.make_async_copy(src, dst, load_sem.at[i])
        for i, (src, dst) in enumerate(
            ((table_hbm, table_v), (win_hbm, win_v), (wout_hbm, wout_v), (cot_hbm, cot_v))
        )
    ]
    for copy in loads:
        copy.start()

    barrier = pltpu.get_barrier_semaphore()
    for peer in ahead:
        pl.semaphore_signal(barrier, inc=1, device_id=(peer, z), device_id_type=MESH)
    for peer in zs:
        pl.semaphore_signal(barrier, inc=1, device_id=(t, peer), device_id_type=MESH)

    names = {}
    pending = []

    def sem(name):
        return names.setdefault(name, len(names))

    def send(src, dst, to, name):
        i = sem(name)
        pltpu.make_async_remote_copy(
            src_ref=src, dst_ref=dst, send_sem=send_sem.at[i], recv_sem=recv_sem.at[i],
            device_id=to, device_id_type=MESH,
        ).start()

    def arrived(ref, name):
        pltpu.make_async_copy(ref, ref, recv_sem.at[sem(name)]).wait()
        pending.append((ref, name))

    for o in range(count):
        for e in range(cap):
            req_s[o, e : e + 1, :] = jnp.full((1, 128), fetch_ref[o, e], jnp.int32)
    pl.semaphore_wait(barrier, count - 1 + nz - 1)
    for k, peer in enumerate(ahead):
        send(req_s.at[peer], req_r.at[k], (peer, z), "list")
    req_r[count - 1] = req_s[t]

    ends = []
    total = jnp.int32(0)
    for s in range(len_ref.shape[1]):
        total = total + len_ref[0, s]
        ends.append(total)
    pos_i = lax.broadcasted_iota(jnp.int32, (tokens, tokens), 0)
    pos_j = lax.broadcasted_iota(jnp.int32, (tokens, tokens), 1)
    first = jnp.zeros((tokens, tokens), jnp.int32)
    for e in ends:
        first = jnp.where(pos_i >= e, e, first)
    allowed[...] = jnp.where((pos_j >= first) & (pos_j <= pos_i), 1.0, 0.0).astype(F32)
    slot_hot = jnp.where(
        lax.broadcasted_iota(jnp.int32, (slots, tokens), 0) == slot_ref[...], 1.0, 0.0
    ).astype(BF)

    arrived(req_r.at[pl.ds(0, count - 1)], "list")
    loads[0].wait()
    lane = lax.broadcasted_iota(jnp.int32, (slots, 128), 1)
    wanted = req_r[...].reshape(slots, 128)
    row_hot = jnp.concatenate(
        [jnp.where(wanted == lane + 128 * i, 1.0, 0.0).astype(BF) for i in range(rows // 128)], axis=1
    )

    def packed(ref, lo, hi):
        ref[...] = jnp.concatenate(
            [lo.reshape(count, cap, half), hi.reshape(count, cap, half)], axis=1
        ).astype(BF)

    def unpacked(ref):
        v = ref[...].astype(F32)
        return jnp.concatenate(
            [v[:, :cap].reshape(slots, half), v[:, cap:].reshape(slots, half)], axis=1
        ).astype(BF)

    packed(found, mm(row_hot, table_v[:, :half]), mm(row_hot, table_v[:, half:]))
    for k, peer in enumerate(behind):
        send(found.at[k], rows_r.at[t], (peer, z), "rows")
    rows_r[t] = found[count - 1]
    loads[1].wait()
    loads[2].wait()
    loads[3].wait()
    arrived(rows_r.at[pl.ds(0, count - 1)], "rows")

    e32 = mm(slot_hot, unpacked(rows_r), TN)
    emb[...] = e32
    cen = e32 - jnp.mean(e32, axis=1, keepdims=True)
    inv_e = lax.rsqrt(jnp.mean(cen * cen, axis=1, keepdims=True) + EPS)
    n32[...] = cen * inv_e
    normed[...] = n32[...].astype(BF)

    def cols(b):
        return slice(b * width, (b + 1) * width)

    for b in range(4):
        p = mm(normed[...], win_v[:, cols(b)])
        sg = jax.nn.sigmoid(p)
        proj[:, cols(b)] = (p * sg).astype(BF)
        dsil[:, cols(b)] = sg * (1.0 + p * (1.0 - sg))

    lanes = lax.broadcasted_iota(jnp.int32, (1, 128), 1)
    side = [
        jnp.where(lanes < 64, 1.0, 0.0).astype(BF),
        jnp.where(lanes >= 64, 1.0, 0.0).astype(BF),
    ]

    def pair(b, i):
        return proj[:, b * width + 128 * i : b * width + 128 * (i + 1)]

    scale = (width // HEADS) ** -0.5
    for i in range(HEADS // 2):
        q, k, v = pair(2, i), pair(3, i), pair(1, i)
        part = None
        for j in range(2):
            s = mm(q, k * side[j], NT) * scale
            sg = jax.nn.sigmoid(s)
            keep = allowed[...]
            w = (keep * (s * sg)).astype(BF)
            weights[2 * i + j] = w
            dfac[2 * i + j] = (keep * scale) * (sg * (1.0 + s * (1.0 - sg)))
            term = mm(w, v * side[j])
            part = term if part is None else part + term
        mixed[:, 128 * i : 128 * (i + 1)] = part

    m32 = mixed[...]
    cen = m32 - jnp.mean(m32, axis=1, keepdims=True)
    inv_m = lax.rsqrt(jnp.mean(cen * cen, axis=1, keepdims=True) + EPS)
    nm = cen * inv_m
    u32 = proj[:, cols(0)].astype(F32)
    gated = (nm * u32).astype(BF)
    cot = cot_v[...]
    out_ref[...] = (emb[...] + mm(gated, wout_v[...])).astype(BF)

    own = rows_of(c * R0, R0)
    other = rows_of((1 - c) * R0, R0)

    def to_partner(b):
        send(g.at[b, other], pr.at[b], (partner, z), f"pair{b}")

    def first_peers(b):
        return (xs, x, ys, y) if b % 2 == 0 else (ys, y, xs, x)

    def plane(v, peers):
        return [plus(v, d, n) for d in range(1, n)]

    def pair_sum(b):
        arrived(pr.at[b], f"pair{b}")
        h[b] = (g[b, own].astype(F32) + pr[b].astype(F32)).astype(BF)
        if b < 4:
            peers, v, _, _ = first_peers(b)
            for k, (peer, place) in enumerate(zip(peers, plane(v, peers))):
                send(h.at[b, rows_of(place * R1, R1)], r1.at[b, k], (peer, z), f"first{b}")
        else:
            for k, place in enumerate(zs):
                send(h.at[b, rows_of(place * (R0 // nz), R0 // nz)], ro1.at[k], (t, place), "o_z")

    def first_sum(b):
        arrived(r1.at[b], f"first{b}")
        _, v, peers, w = first_peers(b)
        acc = h[b, rows_of(v * R1, R1)].astype(F32)
        for k in range(n - 1):
            acc = acc + r1[b, k].astype(F32)
        s1[b] = acc.astype(BF)
        for k, (peer, place) in enumerate(zip(peers, plane(w, peers))):
            send(s1.at[b, rows_of(place * R2, R2)], r2.at[b, k], (peer, z), f"second{b}")

    def second_sum(b):
        arrived(r2.at[b], f"second{b}")
        _, _, _, w = first_peers(b)
        acc = s1[b, rows_of(w * R2, R2)].astype(F32)
        for k in range(n - 1):
            acc = acc + r2[b, k].astype(F32)
        s2[:, cols(b)] = acc.astype(BF)

    d_gated = mm(cot, wout_v[...], NT).astype(BF).astype(F32)
    g[4] = mm(gated, cot, TN).astype(BF)
    to_partner(4)
    normed_t = normed[...].T

    def weight_grad(b, d_proj):
        d = (d_proj.astype(BF).astype(F32) * dsil[:, cols(b)]).astype(BF)
        dpre[:, cols(b)] = d
        g[b] = mm(normed_t, d).astype(BF)
        to_partner(b)

    weight_grad(0, d_gated * nm)
    pair_sum(4)

    gn = d_gated * u32
    dm = inv_m * (
        gn - jnp.mean(gn, axis=1, keepdims=True) - nm * jnp.mean(gn * nm, axis=1, keepdims=True)
    )
    mixed[...] = dm
    d_v = []
    for i in range(HEADS // 2):
        dm_i = mixed[:, 128 * i : 128 * (i + 1)].astype(BF)
        part = None
        for j in range(2):
            term = mm(weights[2 * i + j], dm_i * side[j], TN)
            part = term if part is None else part + term
        d_v.append(part)
    weight_grad(1, jnp.concatenate(d_v, axis=1))
    pair_sum(0)

    d_q, d_k = [], []
    for i in range(HEADS // 2):
        q, k, v = pair(2, i), pair(3, i), pair(1, i)
        dm_i = mixed[:, 128 * i : 128 * (i + 1)].astype(BF)
        part_q = part_k = None
        for j in range(2):
            dw = mm(dm_i, v * side[j], NT).astype(BF).astype(F32)
            ds = (dw * dfac[2 * i + j]).astype(BF)
            term_q = mm(ds, k * side[j])
            term_k = mm(ds, q * side[j], TN)
            part_q = term_q if part_q is None else part_q + term_q
            part_k = term_k if part_k is None else part_k + term_k
        d_q.append(part_q)
        d_k.append(part_k)
    weight_grad(2, jnp.concatenate(d_q, axis=1))
    weight_grad(3, jnp.concatenate(d_k, axis=1))
    pair_sum(1)
    pair_sum(2)
    pair_sum(3)

    dn = mm(dpre[...], win_v[...], NT).astype(BF).astype(F32)
    first_sum(0)
    first_sum(1)
    nv = n32[...]
    de = cot.astype(F32) + inv_e * (
        dn - jnp.mean(dn, axis=1, keepdims=True) - nv * jnp.mean(dn * nv, axis=1, keepdims=True)
    )
    sg32 = mm(slot_hot, de.astype(BF))
    packed(sg_s, sg32[:, :half], sg32[:, half:])
    for k, peer in enumerate(ahead):
        send(sg_s.at[peer], sg_r.at[k], (peer, z), "slot")
    sg_r[count - 1] = sg_s[t]

    RZ = R0 // nz
    CX = width // n
    arrived(ro1, "o_z")
    acc = h[4, rows_of(z * RZ, RZ)].astype(F32)
    for k in range(nz - 1):
        acc = acc + ro1[k].astype(F32)
    h[4, rows_of(z * RZ, RZ)] = acc.astype(BF)
    for k, (peer, place) in enumerate(zip(xs, plane(x, xs))):
        send(
            h.at[4, rows_of(z * RZ, RZ), rows_of(place * CX, CX)], ro2.at[k], (peer, z), "o_x"
        )
    first_sum(2)
    first_sum(3)
    arrived(ro2, "o_x")
    acc = h[4, rows_of(z * RZ, RZ), rows_of(x * CX, CX)].astype(F32)
    for k in range(n - 1):
        acc = acc + ro2[k].astype(F32)
    so2[...] = acc.astype(BF)
    ro3[y] = so2[...]
    for peer in ys:
        send(so2, ro3.at[y], (peer, z), "o_y")
    for b in range(4):
        second_sum(b)

    for k, place in enumerate(zs):
        send(s2.at[:, rows_of(place * CZ, CZ)], r3.at[k], (t, place), "last")

    arrived(sg_r.at[pl.ds(0, count - 1)], "slot")
    tg_ref[...] = mm(row_hot, unpacked(sg_r), TN).astype(BF)

    arrived(ro3.at[pl.ds(0, n - 1)], "o_y")
    acc = ro3[0].astype(F32)
    for k in range(1, n):
        acc = acc + ro3[k].astype(F32)
    orow = c * R0 + z * RZ
    ocol = rows_of(x * CX, CX)
    fullo_ref[rows_of(orow, RZ), ocol] = acc.astype(BF)
    for peer in xs:
        strip = fullo_ref.at[rows_of(orow, RZ), ocol]
        send(strip, strip, (peer, z), "o_gx")

    arrived(r3, "last")
    zcols = rows_of(z * CZ, CZ)
    acc = s2[:, zcols].astype(F32)
    for k in range(nz - 1):
        acc = acc + r3[k].astype(F32)
    a2[:, zcols] = acc.astype(BF)
    for peer in zs:
        send(a2.at[:, zcols], a2.at[:, zcols], (t, peer), "g_z")

    arrived(ro2, "o_gx")
    for peer in zs:
        strip = fullo_ref.at[rows_of(orow, RZ)]
        send(strip, strip, (t, peer), "o_gz")

    arrived(a2.at[:, pl.ds(0, CZ * (nz - 1))], "g_z")
    strips = []
    for b in range(4):
        _, v, peers, w = first_peers(b)
        base = c * R0 + v * R1
        strips.append((base, v))
        mine = rows_of(base + w * R2, R2)
        full_ref[mine, cols(b)] = a2[:, cols(b)]
        for peer in peers:
            strip = full_ref.at[mine, cols(b)]
            send(strip, strip, (peer, z), f"g_second{b}")
    arrived(ro1, "o_gz")
    strip = fullo_ref.at[own]
    send(strip, strip, (partner, z), "o_gp")
    for b in range(4):
        arrived(r2.at[b], f"g_second{b}")
        peers, _, _, _ = first_peers(b)
        base, v = strips[b]
        strip = full_ref.at[rows_of(base, R1), cols(b)]
        for k, peer in enumerate(peers):
            send(strip, strip, (peer, z), f"g_first{b}_{k}")
        send(strip, strip, (partner, z), f"g_pair{b}_{n - 1}")
    for k in range(n - 1):
        for b in range(4):
            arrived(s1.at[b], f"g_first{b}_{k}")
            _, v, _, _ = first_peers(b)
            place = plus(v, n - 1 - k, n)
            strip = full_ref.at[rows_of(c * R0 + place * R1, R1), cols(b)]
            send(strip, strip, (partner, z), f"g_pair{b}_{k}")
    arrived(fullo_ref.at[other], "o_gp")
    for k in range(n):
        for b in range(4):
            arrived(s1.at[b], f"g_pair{b}_{(k + n - 1) % n}")

    for ref, name in pending:
        pltpu.make_async_copy(ref, ref, send_sem.at[sem(name)]).wait()
    assert len(names) <= send_sem.shape[0]


def body(n, nz, table, fetch_rows, item_slot, seq_lengths, w_in, w_out, out_cot):
    _, count, cap = fetch_rows.shape
    rows, width = table.shape
    tokens = item_slot.shape[0]
    slots = count * cap
    half = width // 2
    R0 = width // 2
    R1 = R0 // n
    R2 = R1 // n
    CZ = 4 * width // nz
    any_ = pl.BlockSpec(memory_space=pl.ANY)
    vmem = pl.BlockSpec(memory_space=pltpu.VMEM)
    smem = pl.BlockSpec(memory_space=pltpu.SMEM)
    V = pltpu.VMEM
    layer_out, table_grad, sum_in, sum_out = pl.pallas_call(
        functools.partial(kernel, n, nz, count, cap, rows, tokens, width),
        out_shape=(
            jax.ShapeDtypeStruct((tokens, width), BF),
            jax.ShapeDtypeStruct((rows, width), BF),
            jax.ShapeDtypeStruct((width, 4 * width), BF),
            jax.ShapeDtypeStruct((width, width), BF),
        ),
        in_specs=[smem, vmem, smem, any_, any_, any_, any_],
        out_specs=(vmem, vmem, vmem, vmem),
        scratch_shapes=[
            V((rows, width), BF), V((width, 4 * width), BF), V((width, width), BF), V((tokens, width), BF),
            V((count, cap, 128), jnp.int32), V((count, cap, 128), jnp.int32),
            V((count, 2 * cap, half), BF), V((count, 2 * cap, half), BF),
            V((count, 2 * cap, half), BF), V((count, 2 * cap, half), BF),
            V((tokens, width), F32), V((tokens, width), F32), V((tokens, width), BF),
            V((tokens, 4 * width), BF), V((tokens, 4 * width), F32), V((tokens, 4 * width), BF),
            V((HEADS, tokens, tokens), BF), V((HEADS, tokens, tokens), F32),
            V((tokens, width), F32), V((tokens, tokens), F32),
            V((5, width, width), BF), V((5, R0, width), BF), V((5, R0, width), BF),
            V((4, n - 1, R1, width), BF), V((4, R1, width), BF),
            V((4, n - 1, R2, width), BF), V((R2, 4 * width), BF),
            V((nz - 1, R2, CZ), BF), V((R2, 4 * width), BF),
            V((nz - 1, R0 // nz, width), BF), V((n - 1, R0 // nz, width // n), BF),
            V((R0 // nz, width // n), BF), V((n, R0 // nz, width // n), BF),
            pltpu.SemaphoreType.DMA((4,)),
            pltpu.SemaphoreType.DMA((64,)),
            pltpu.SemaphoreType.DMA((64,)),
        ],
        compiler_params=pltpu.CompilerParams(
            collective_id=0, has_side_effects=True, vmem_limit_bytes=56 * 1024 * 1024
        ),
    )(
        fetch_rows.reshape(count, cap), item_slot.reshape(1, tokens), seq_lengths,
        table, w_in, w_out, out_cot,
    )
    grad_scale = float(tokens * count * nz) ** (-0.5)
    return (
        layer_out,
        table_grad[None],
        sum_in.astype(F32) * grad_scale,
        sum_out.astype(F32) * grad_scale,
    )


def solution(mesh):
    placed = (
        P("table", None),
        P(("table", "group"), None, None),
        P(("table", "group")),
        P(("table", "group"), None),
        P(),
        P(),
        P(("table", "group"), None),
    )
    n = math.isqrt(mesh.shape["table"] // 2)
    return jax.shard_map(
        functools.partial(body, n, mesh.shape["group"]),
        mesh=mesh,
        in_specs=placed,
        out_specs=(P(("table", "group"), None), P("group", "table", None), P(), P()),
        check_vma=False,
    )
```

time: 354 us -> 80.6 us (0.23)
  waiting for transfers between devices: 271 us -> 0 us
  Pallas kernels: 0 us -> 71.3 us
  matrix products: 27 us -> 0 us
  starting transfers between devices: 16.5 us -> 0 us
  between operations: 14.3 us -> 0.67 us
  local copies, waits for them, and re-layouts: 11.6 us -> 3.05 us
  other arithmetic: 12.8 us -> 5.4 us
    psum x1 -> x0, waiting for transfers between devices: 249 us -> none  [body(): lax.psum((grad_in.astype(jnp.float32), grad_out.astype(jnp.float32)), ('t...]
    pallas_call x0 -> x1, Pallas kernels: none -> 71.3 us  [body(): pl.pallas_call(functools.partial(kernel, n, nz, count, cap, rows, tokens,...]
    dot_general x14 -> x0, matrix products: 27 us -> none  [the longest x3 10.5 us: hstu_layer(): jnp.dot(normed, w_in, preferred_element_type=jnp.float32)]
    all_to_all x3 -> x0, waiting for transfers between devices: 21.7 us -> none  [the longest x1 8.93 us: body(): lax.all_to_all(found, 'table', split_axis=0, concat_axis=1, tiled=True)]
    all_to_all x3 -> x0, starting transfers between devices: 16.5 us -> none  [the longest x1 8.59 us: body(): lax.all_to_all(fetch_rows, 'table', split_axis=1, concat_axis=0, tiled=True)]
    gather x2 -> x0, local copies, waits for them, and re-layouts: 3.72 us -> none  [the longest x1 2.57 us: body(): found = jnp.take(table, requested, axis=0)]
    reshape x4 -> x0, local copies, waits for them, and re-layouts: 3.7 us -> none  [the longest x1 1.84 us: hstu_layer(): key_heads = projected[:, 3 * width:].reshape(token_count, HEADS, head_dim)]
  transfers between devices with their start and end apart: 4 -> 0, of which waited for: 4 -> 0; matrix products, arithmetic and copies ran while one was open for 3% -> 0% of each run, Pallas kernels for 0% -> 0%
where the time goes in v1:
time: 80.6 us; the launch traced here: 80.4 us
  Pallas kernels  71.3 us (88%)
  other arithmetic  5.4 us (7%)
  local copies, waits for them, and re-layouts  3.05 us (4%)
    pallas_call x1, Pallas kernels, body(): pl.pallas_call(functools.partial(kernel, n, nz, count, cap, rows, tokens,...  71.3 us
    mul x1, other arithmetic, body(): sum_in.astype(F32) * grad_scale  4.29 us
    unnamed x9, local copies, waits for them, and re-layouts  3.05 us

profile of v1, /device:TPU:1, one launch (start us, length us, event | category | flops | bytes accessed | tf_op | source)
XLA Modules:
  0.0 80.4 jit_solution(2228477150801778043)
XLA Ops:
  0.6 1.4 %copy.11 = s32[1,32,8]{2,1,0:T(8,128)} copy(s32[1,32,8]{1,2,0:T(8,128)} %param.8) | data formatting | bytes 2048 | tf_op args[1]
  2.0 71.3 %shard_map.102 = (bf16[256,512]{1,0:T(8,128)(2,1)}, bf16[1024,512]{1,0:T(8,128)(2,1)}, bf16[512,2048]{1,0:T(8,128)(2,1)}, bf16[512,512]{1,0:T(8,128)(2,1)}) custom-call(s32[32,8]{1,0:T(8,128)} %bitcast.4, s32[1,256]{1,0:T(1,128)} %bitcast.5, s32[1,8]{1,0:T(1,128)} %len_ref.1, bf16[1024,512]{1,0:T(8,128)(2,1)} %table_hbm.1, bf16[512,2048]{1,0:T(8,128)(2,1)} %win_hbm.1, ...), custom_call_target="tpu_custom_call" | custom-call | tf_op jit(solution)/shard_map/pallas_call | solution.py:411
  73.3 0.0 copy-start.1
  73.3 0.0 copy-start.2
  73.3 0.0 copy-start
  73.3 4.3 %convert_multiply_fusion = f32[512,2048]{1,0:T(8,128)} fusion(bf16[512,2048]{1,0:T(8,128)(2,1)} %get-tuple-element.10), kind=kLoop, calls=%fused_computation | loop fusion | flops 2097152 | bytes 6291456 | tf_op jit(solution)/shard_map/mul | solution.py:451
  77.6 0.0 copy-done.1
  77.6 1.1 %convert_multiply_fusion.1 = f32[512,512]{1,0:T(8,128)} fusion(bf16[512,512]{1,0:T(8,128)(2,1)S(1)} %copy-done.1), kind=kLoop, calls=%fused_computation.1 | loop fusion | flops 524288 | bytes 1572864 | tf_op jit(solution)/shard_map/mul | solution.py:452
  78.7 0.0 copy-done.2
  78.7 0.7 copy.14
  79.4 0.0 copy-done
  79.4 1.0 %copy.15 = bf16[1,1024,512]{2,1,0:T(8,128)(2,1)} copy(bf16[1,1024,512]{2,1,0:T(8,128)(2,1)S(1)} %bitcast.3) | data formatting | bytes 2097152
Async XLA Ops:
  73.3 4.3 %copy-start.1 = (bf16[512,512]{1,0:T(8,128)(2,1)S(1)}, bf16[512,512]{1,0:T(8,128)(2,1)}, u32[]{:S(2)}) copy-start(bf16[512,512]{1,0:T(8,128)(2,1)} %get-tuple-element.11) | copy-start | bytes 1572868
  73.3 5.4 %copy-start.2 = (bf16[256,512]{1,0:T(8,128)(2,1)S(1)}, bf16[256,512]{1,0:T(8,128)(2,1)}, u32[]{:S(2)}) copy-start(bf16[256,512]{1,0:T(8,128)(2,1)} %get-tuple-element.16) | copy-start | bytes 786436
  73.3 6.1 %copy-start = (bf16[1024,512]{1,0:T(8,128)(2,1)S(1)}, bf16[1024,512]{1,0:T(8,128)(2,1)}, u32[]{:S(2)}) copy-start(bf16[1024,512]{1,0:T(8,128)(2,1)} %get-tuple-element.9) | copy-start | bytes 3145732

commit v2 on v1

--- a/solution.py
+++ b/solution.py
@@ -28,14 +28,14 @@
 
 
 def kernel(
-    n, nz, count, cap, rows, tokens, width,
-    fetch_ref, slot_ref, len_ref, table_hbm, win_hbm, wout_hbm, cot_hbm,
-    out_ref, tg_ref, full_ref, fullo_ref,
-    table_v, win_v, wout_v, cot_v,
+    n, nz, count, cap, rows, tokens, width, grad_scale,
+    fetch_hbm, slot_hbm, len_hbm, table_hbm, win_hbm, wout_hbm, cot_hbm,
+    out_ref, tg_ref, gin_ref, gout_ref,
+    fetch_ref, slot_ref, len_ref, table_v, win_v, wout_v, cot_v,
     req_s, req_r, found, rows_r, sg_s, sg_r,
-    emb, n32, normed, proj, dsil, dpre, weights, dfac, mixed, allowed,
+    row_hot, emb, n32, normed, proj, dsil, dpre, weights, dfac, mixed, allowed,
     g, pr, h, r1, s1, r2, s2, r3, a2,
-    ro1, ro2, so2, ro3,
+    ro1, ro2, so2, ro3, full_ref, fullo_ref,
     load_sem, send_sem, recv_sem,
 ):
     t = lax.axis_index("table")
@@ -48,7 +48,7 @@
     R0 = width // 2
     R1 = R0 // n
     R2 = R1 // n
-    CZ = 4 * width // nz
+    CZ = 2 * width // nz
 
     def at(px, py, pc):
         return (px * n + py) * 2 + pc
@@ -56,18 +56,27 @@
     def plus(v, d, m):
         return lax.rem(v + d, m)
 
+    def far(d, m):
+        return min(d, m - d)
+
     offsets = [(dx, dy, dc) for dx in range(n) for dy in range(n) for dc in range(2)][1:]
+    offsets.sort(key=lambda o: (-far(o[0], n) - far(o[1], n), o))
+    steps = sorted(range(1, n), key=lambda d: -far(d, n))
+    zsteps = sorted(range(1, nz), key=lambda d: -far(d, nz))
     ahead = [at(plus(x, dx, n), plus(y, dy, n), plus(c, dc, 2)) for dx, dy, dc in offsets]
     behind = [at(plus(x, n - dx, n), plus(y, n - dy, n), plus(c, 2 - dc, 2)) for dx, dy, dc in offsets]
-    zs = [plus(z, d, nz) for d in range(1, nz)]
-    xs = [at(plus(x, d, n), y, c) for d in range(1, n)]
-    ys = [at(x, plus(y, d, n), c) for d in range(1, n)]
+    zs = [plus(z, d, nz) for d in zsteps]
+    xs = [at(plus(x, d, n), y, c) for d in steps]
+    ys = [at(x, plus(y, d, n), c) for d in steps]
     partner = at(x, y, 1 - c)
 
     loads = [
         pltpu.make_async_copy(src, dst, load_sem.at[i])
         for i, (src, dst) in enumerate(
-            ((table_hbm, table_v), (win_hbm, win_v), (wout_hbm, wout_v), (cot_hbm, cot_v))
+            (
+                (fetch_hbm, fetch_ref), (len_hbm, len_ref), (slot_hbm, slot_ref),
+                (table_hbm, table_v), (win_hbm, win_v), (wout_hbm, wout_v), (cot_hbm, cot_v),
+            )
         )
     ]
     for copy in loads:
@@ -96,14 +105,20 @@
         pltpu.make_async_copy(ref, ref, recv_sem.at[sem(name)]).wait()
         pending.append((ref, name))
 
+    loads[0].wait()
+    lane = lax.broadcasted_iota(jnp.int32, (1, 128), 1)
     for o in range(count):
+        line = jnp.zeros((1, 128), jnp.int32)
         for e in range(cap):
-            req_s[o, e : e + 1, :] = jnp.full((1, 128), fetch_ref[o, e], jnp.int32)
+            line = jnp.where(lane == e, fetch_ref[e, o], line)
+        req_s[o] = line
     pl.semaphore_wait(barrier, count - 1 + nz - 1)
     for k, peer in enumerate(ahead):
-        send(req_s.at[peer], req_r.at[k], (peer, z), "list")
+        send(req_s.at[peer], req_r.at[k], (peer, z), f"list{0 if k < count // 2 else count // 2}")
     req_r[count - 1] = req_s[t]
 
+    loads[1].wait()
+    loads[2].wait()
     ends = []
     total = jnp.int32(0)
     for s in range(len_ref.shape[1]):
@@ -119,18 +134,19 @@
         lax.broadcasted_iota(jnp.int32, (slots, tokens), 0) == slot_ref[...], 1.0, 0.0
     ).astype(BF)
 
-    arrived(req_r.at[pl.ds(0, count - 1)], "list")
-    loads[0].wait()
-    lane = lax.broadcasted_iota(jnp.int32, (slots, 128), 1)
-    wanted = req_r[...].reshape(slots, 128)
-    row_hot = jnp.concatenate(
-        [jnp.where(wanted == lane + 128 * i, 1.0, 0.0).astype(BF) for i in range(rows // 128)], axis=1
-    )
-
-    def packed(ref, lo, hi):
-        ref[...] = jnp.concatenate(
-            [lo.reshape(count, cap, half), hi.reshape(count, cap, half)], axis=1
-        ).astype(BF)
+    def hot_rows(start, size):
+        lists = jnp.broadcast_to(req_r[start : start + size].astype(F32), (size, cap, 128))
+        diagonal = lax.broadcasted_iota(jnp.int32, (size, cap, 128), 1) == lax.broadcasted_iota(
+            jnp.int32, (size, cap, 128), 2
+        )
+        wanted = jnp.sum(jnp.where(diagonal, lists, 0.0), axis=2, keepdims=True).reshape(size * cap, 1)
+        lane = lax.broadcasted_iota(jnp.int32, (size * cap, 128), 1).astype(F32)
+        row_hot[start * cap : (start + size) * cap] = jnp.concatenate(
+            [jnp.where(wanted == lane + 128.0 * i, 1.0, 0.0).astype(BF) for i in range(rows // 128)], axis=1
+        )
+
+    def packed(lo, hi):
+        return jnp.concatenate([lo.reshape(-1, cap, half), hi.reshape(-1, cap, half)], axis=1).astype(BF)
 
     def unpacked(ref):
         v = ref[...].astype(F32)
@@ -138,13 +154,19 @@
             [v[:, :cap].reshape(slots, half), v[:, cap:].reshape(slots, half)], axis=1
         ).astype(BF)
 
-    packed(found, mm(row_hot, table_v[:, :half]), mm(row_hot, table_v[:, half:]))
-    for k, peer in enumerate(behind):
-        send(found.at[k], rows_r.at[t], (peer, z), "rows")
+    cut = count // 2
+    for start, size, got in ((cut, cut, cut - 1), (0, cut, cut)):
+        arrived(req_r.at[pl.ds(start, got)], f"list{start}")
+        if start:
+            loads[3].wait()
+        hot_rows(start, size)
+        hot = row_hot[start * cap : (start + size) * cap]
+        found[start : start + size] = packed(mm(hot, table_v[:, :half]), mm(hot, table_v[:, half:]))
+        for k in range(start, start + got):
+            send(found.at[k], rows_r.at[t], (behind[k], z), "rows")
     rows_r[t] = found[count - 1]
-    loads[1].wait()
-    loads[2].wait()
-    loads[3].wait()
+    for i in (4, 5, 6):
+        loads[i].wait()
     arrived(rows_r.at[pl.ds(0, count - 1)], "rows")
 
     e32 = mm(slot_hot, unpacked(rows_r), TN)
@@ -159,7 +181,7 @@
 
     for b in range(4):
         p = mm(normed[...], win_v[:, cols(b)])
-        sg = jax.nn.sigmoid(p)
+        sg = 0.5 + 0.5 * jnp.tanh(0.5 * p)
         proj[:, cols(b)] = (p * sg).astype(BF)
         dsil[:, cols(b)] = sg * (1.0 + p * (1.0 - sg))
 
@@ -178,7 +200,7 @@
         part = None
         for j in range(2):
             s = mm(q, k * side[j], NT) * scale
-            sg = jax.nn.sigmoid(s)
+            sg = 0.5 + 0.5 * jnp.tanh(0.5 * s)
             keep = allowed[...]
             w = (keep * (s * sg)).astype(BF)
             weights[2 * i + j] = w
@@ -206,7 +228,7 @@
         return (xs, x, ys, y) if b % 2 == 0 else (ys, y, xs, x)
 
     def plane(v, peers):
-        return [plus(v, d, n) for d in range(1, n)]
+        return [plus(v, d, n) for d in steps]
 
     def pair_sum(b):
         arrived(pr.at[b], f"pair{b}")
@@ -235,7 +257,59 @@
         acc = s1[b, rows_of(w * R2, R2)].astype(F32)
         for k in range(n - 1):
             acc = acc + r2[b, k].astype(F32)
-        s2[:, cols(b)] = acc.astype(BF)
+        s2[b // 2, :, cols(b % 2)] = acc.astype(BF)
+        if b % 2 == 1:
+            for k, place in enumerate(zs):
+                send(
+                    s2.at[b // 2, :, rows_of(place * CZ, CZ)], r3.at[b // 2, k], (t, place), f"last{b // 2}"
+                )
+
+    zcols = rows_of(z * CZ, CZ)
+
+    def last_sum(i):
+        arrived(r3.at[i], f"last{i}")
+        acc = s2[i, :, zcols].astype(F32)
+        for k in range(nz - 1):
+            acc = acc + r3[i, k].astype(F32)
+        a2[i, :, zcols] = acc.astype(BF)
+        for peer in zs:
+            send(a2.at[i, :, zcols], a2.at[i, :, zcols], (t, peer), f"g_z{i}")
+
+    def back_z(i):
+        arrived(a2.at[i, :, pl.ds(0, CZ * (nz - 1))], f"g_z{i}")
+        for b in (2 * i, 2 * i + 1):
+            _, v, peers, w = first_peers(b)
+            mine = rows_of(c * R0 + v * R1 + w * R2, R2)
+            full_ref[mine, cols(b)] = a2[i, :, cols(b % 2)]
+            for peer in peers:
+                strip = full_ref.at[mine, cols(b)]
+                send(strip, strip, (peer, z), f"g_second{b}")
+
+    def back_second(b):
+        arrived(r2.at[b], f"g_second{b}")
+        peers, v, _, _ = first_peers(b)
+        strip = full_ref.at[rows_of(c * R0 + v * R1, R1), cols(b)]
+        for k, peer in enumerate(peers):
+            send(strip, strip, (peer, z), f"g_first{b}_{k}")
+        send(strip, strip, (partner, z), f"g_pair{b}_{n - 1}")
+
+    def strip_of(core, b, k):
+        _, v, _, _ = first_peers(b)
+        place = plus(v, n - steps[k], n) if k < n - 1 else v
+        return rows_of(core * R0 + place * R1, R1)
+
+    def finish(core, b, k):
+        strip = strip_of(core, b, k)
+        gin_ref[strip, cols(b)] = full_ref[strip, cols(b)].astype(F32) * grad_scale
+
+    def back_first(b, k):
+        arrived(s1.at[b], f"g_first{b}_{k}")
+        strip = full_ref.at[strip_of(c, b, k), cols(b)]
+        send(strip, strip, (partner, z), f"g_pair{b}_{k}")
+
+    def back_pair(b, k):
+        arrived(s1.at[b], f"g_pair{b}_{k}")
+        finish(1 - c, b, k)
 
     d_gated = mm(cot, wout_v[...], NT).astype(BF).astype(F32)
     g[4] = mm(gated, cot, TN).astype(BF)
@@ -281,9 +355,10 @@
             part_k = term_k if part_k is None else part_k + term_k
         d_q.append(part_q)
         d_k.append(part_k)
+        if i == 0:
+            pair_sum(1)
     weight_grad(2, jnp.concatenate(d_q, axis=1))
     weight_grad(3, jnp.concatenate(d_k, axis=1))
-    pair_sum(1)
     pair_sum(2)
     pair_sum(3)
 
@@ -295,9 +370,7 @@
         dn - jnp.mean(dn, axis=1, keepdims=True) - nv * jnp.mean(dn * nv, axis=1, keepdims=True)
     )
     sg32 = mm(slot_hot, de.astype(BF))
-    packed(sg_s, sg32[:, :half], sg32[:, half:])
-    for k, peer in enumerate(ahead):
-        send(sg_s.at[peer], sg_r.at[k], (peer, z), "slot")
+    sg_s[...] = packed(sg32[:, :half], sg32[:, half:])
     sg_r[count - 1] = sg_s[t]
 
     RZ = R0 // nz
@@ -311,6 +384,8 @@
         send(
             h.at[4, rows_of(z * RZ, RZ), rows_of(place * CX, CX)], ro2.at[k], (peer, z), "o_x"
         )
+    second_sum(0)
+    second_sum(1)
     first_sum(2)
     first_sum(3)
     arrived(ro2, "o_x")
@@ -321,77 +396,82 @@
     ro3[y] = so2[...]
     for peer in ys:
         send(so2, ro3.at[y], (peer, z), "o_y")
-    for b in range(4):
-        second_sum(b)
-
-    for k, place in enumerate(zs):
-        send(s2.at[:, rows_of(place * CZ, CZ)], r3.at[k], (t, place), "last")
-
-    arrived(sg_r.at[pl.ds(0, count - 1)], "slot")
-    tg_ref[...] = mm(row_hot, unpacked(sg_r), TN).astype(BF)
+    second_sum(2)
+    second_sum(3)
+    for k, peer in enumerate(ahead):
+        send(sg_s.at[peer], sg_r.at[k], (peer, z), "slot")
+    last_sum(0)
 
     arrived(ro3.at[pl.ds(0, n - 1)], "o_y")
     acc = ro3[0].astype(F32)
     for k in range(1, n):
         acc = acc + ro3[k].astype(F32)
-    orow = c * R0 + z * RZ
-    ocol = rows_of(x * CX, CX)
-    fullo_ref[rows_of(orow, RZ), ocol] = acc.astype(BF)
+    orows = rows_of(c * R0 + z * RZ, RZ)
+    ocols = rows_of(x * CX, CX)
+    fullo_ref[orows, ocols] = acc.astype(BF)
     for peer in xs:
-        strip = fullo_ref.at[rows_of(orow, RZ), ocol]
+        strip = fullo_ref.at[orows, ocols]
         send(strip, strip, (peer, z), "o_gx")
 
-    arrived(r3, "last")
-    zcols = rows_of(z * CZ, CZ)
-    acc = s2[:, zcols].astype(F32)
-    for k in range(nz - 1):
-        acc = acc + r3[k].astype(F32)
-    a2[:, zcols] = acc.astype(BF)
-    for peer in zs:
-        send(a2.at[:, zcols], a2.at[:, zcols], (t, peer), "g_z")
-
+    last_sum(1)
     arrived(ro2, "o_gx")
     for peer in zs:
-        strip = fullo_ref.at[rows_of(orow, RZ)]
+        strip = fullo_ref.at[orows]
         send(strip, strip, (t, peer), "o_gz")
-
-    arrived(a2.at[:, pl.ds(0, CZ * (nz - 1))], "g_z")
-    strips = []
+    back_z(0)
+    arrived(sg_r.at[pl.ds(0, count - 1)], "slot")
+    tg_ref[...] = mm(row_hot[...], unpacked(sg_r), TN).astype(BF)
+    back_z(1)
+    back_second(0)
+    back_second(1)
+    back_second(2)
+    back_second(3)
     for b in range(4):
-        _, v, peers, w = first_peers(b)
-        base = c * R0 + v * R1
-        strips.append((base, v))
-        mine = rows_of(base + w * R2, R2)
-        full_ref[mine, cols(b)] = a2[:, cols(b)]
-        for peer in peers:
-            strip = full_ref.at[mine, cols(b)]
-            send(strip, strip, (peer, z), f"g_second{b}")
+        finish(c, b, n - 1)
+    for k in reversed(range(n - 1)):
+        back_first(0, k)
+        back_first(1, k)
     arrived(ro1, "o_gz")
     strip = fullo_ref.at[own]
     send(strip, strip, (partner, z), "o_gp")
+    for b in range(2):
+        for k in range(n - 1):
+            finish(c, b, k)
+    gout_ref[own] = fullo_ref[own].astype(F32) * grad_scale
     for b in range(4):
-        arrived(r2.at[b], f"g_second{b}")
-        peers, _, _, _ = first_peers(b)
-        base, v = strips[b]
-        strip = full_ref.at[rows_of(base, R1), cols(b)]
-        for k, peer in enumerate(peers):
-            send(strip, strip, (peer, z), f"g_first{b}_{k}")
-        send(strip, strip, (partner, z), f"g_pair{b}_{n - 1}")
-    for k in range(n - 1):
-        for b in range(4):
-            arrived(s1.at[b], f"g_first{b}_{k}")
-            _, v, _, _ = first_peers(b)
-            place = plus(v, n - 1 - k, n)
-            strip = full_ref.at[rows_of(c * R0 + place * R1, R1), cols(b)]
-            send(strip, strip, (partner, z), f"g_pair{b}_{k}")
+        back_pair(b, n - 1)
+    for k in reversed(range(n - 1)):
+        back_pair(0, k)
+        back_pair(1, k)
+    for k in reversed(range(n - 1)):
+        back_first(2, k)
+        back_first(3, k)
+        finish(c, 2, k)
+        finish(c, 3, k)
     arrived(fullo_ref.at[other], "o_gp")
-    for k in range(n):
-        for b in range(4):
-            arrived(s1.at[b], f"g_pair{b}_{(k + n - 1) % n}")
+    gout_ref[other] = fullo_ref[other].astype(F32) * grad_scale
+    for k in reversed(range(n - 1)):
+        back_pair(2, k)
+        back_pair(3, k)
 
     for ref, name in pending:
         pltpu.make_async_copy(ref, ref, send_sem.at[sem(name)]).wait()
     assert len(names) <= send_sem.shape[0]
+
+
+def store(*refs):
+    sems = refs[-1]
+    copies = []
+    for src, dst in zip(refs[:4], refs[4:8]):
+        parts = 8 if src.dtype == F32 and src.shape[1] > src.shape[0] else 2
+        size = src.shape[0] // parts
+        for i in range(parts):
+            part = pl.ds(i * size, size)
+            copies.append(pltpu.make_async_copy(src.at[part], dst.at[part], sems.at[len(copies)]))
+    for copy in copies:
+        copy.start()
+    for copy in copies:
+        copy.wait()
 
 
 def body(n, nz, table, fetch_rows, item_slot, seq_lengths, w_in, w_out, out_cot):
@@ -403,54 +483,61 @@
     R0 = width // 2
     R1 = R0 // n
     R2 = R1 // n
-    CZ = 4 * width // nz
+    CZ = 2 * width // nz
     any_ = pl.BlockSpec(memory_space=pl.ANY)
     vmem = pl.BlockSpec(memory_space=pltpu.VMEM)
-    smem = pl.BlockSpec(memory_space=pltpu.SMEM)
+    hbm = pl.BlockSpec(memory_space=pltpu.HBM)
     V = pltpu.VMEM
-    layer_out, table_grad, sum_in, sum_out = pl.pallas_call(
-        functools.partial(kernel, n, nz, count, cap, rows, tokens, width),
+    grad_scale = float(tokens * count * nz) ** (-0.5)
+    made = pl.pallas_call(
+        functools.partial(kernel, n, nz, count, cap, rows, tokens, width, grad_scale),
         out_shape=(
-            jax.ShapeDtypeStruct((tokens, width), BF),
-            jax.ShapeDtypeStruct((rows, width), BF),
-            jax.ShapeDtypeStruct((width, 4 * width), BF),
-            jax.ShapeDtypeStruct((width, width), BF),
+            V((tokens, width), BF), V((rows, width), BF), V((width, 4 * width), F32), V((width, width), F32),
         ),
-        in_specs=[smem, vmem, smem, any_, any_, any_, any_],
+        in_specs=[hbm] * 7,
         out_specs=(vmem, vmem, vmem, vmem),
         scratch_shapes=[
+            pltpu.SMEM((cap, count), jnp.int32), V((1, tokens), jnp.int32), pltpu.SMEM(seq_lengths.shape, jnp.int32),
             V((rows, width), BF), V((width, 4 * width), BF), V((width, width), BF), V((tokens, width), BF),
-            V((count, cap, 128), jnp.int32), V((count, cap, 128), jnp.int32),
+            V((count, 1, 128), jnp.int32), V((count, 1, 128), jnp.int32),
             V((count, 2 * cap, half), BF), V((count, 2 * cap, half), BF),
             V((count, 2 * cap, half), BF), V((count, 2 * cap, half), BF),
-            V((tokens, width), F32), V((tokens, width), F32), V((tokens, width), BF),
+            V((slots, rows), BF), V((tokens, width), F32), V((tokens, width), F32), V((tokens, width), BF),
             V((tokens, 4 * width), BF), V((tokens, 4 * width), F32), V((tokens, 4 * width), BF),
             V((HEADS, tokens, tokens), BF), V((HEADS, tokens, tokens), F32),
             V((tokens, width), F32), V((tokens, tokens), F32),
             V((5, width, width), BF), V((5, R0, width), BF), V((5, R0, width), BF),
             V((4, n - 1, R1, width), BF), V((4, R1, width), BF),
-            V((4, n - 1, R2, width), BF), V((R2, 4 * width), BF),
-            V((nz - 1, R2, CZ), BF), V((R2, 4 * width), BF),
+            V((4, n - 1, R2, width), BF), V((2, R2, 2 * width), BF),
+            V((2, nz - 1, R2, CZ), BF), V((2, R2, 2 * width), BF),
             V((nz - 1, R0 // nz, width), BF), V((n - 1, R0 // nz, width // n), BF),
             V((R0 // nz, width // n), BF), V((n, R0 // nz, width // n), BF),
-            pltpu.SemaphoreType.DMA((4,)),
+            V((width, 4 * width), BF), V((width, width), BF),
+            pltpu.SemaphoreType.DMA((7,)),
             pltpu.SemaphoreType.DMA((64,)),
             pltpu.SemaphoreType.DMA((64,)),
         ],
         compiler_params=pltpu.CompilerParams(
-            collective_id=0, has_side_effects=True, vmem_limit_bytes=56 * 1024 * 1024
+            collective_id=0, has_side_effects=True, vmem_limit_bytes=40 * 1024 * 1024
         ),
     )(
-        fetch_rows.reshape(count, cap), item_slot.reshape(1, tokens), seq_lengths,
-        table, w_in, w_out, out_cot,
+        *(
+            pltpu.with_memory_space_constraint(v, pltpu.HBM)
+            for v in (
+                fetch_rows[0].T, item_slot.reshape(1, tokens), seq_lengths, table, w_in, w_out, out_cot
+            )
+        )
     )
-    grad_scale = float(tokens * count * nz) ** (-0.5)
-    return (
-        layer_out,
-        table_grad[None],
-        sum_in.astype(F32) * grad_scale,
-        sum_out.astype(F32) * grad_scale,
-    )
+    made = [pltpu.with_memory_space_constraint(v, pltpu.VMEM) for v in made]
+    layer_out, table_grad, sum_in, sum_out = pl.pallas_call(
+        store,
+        out_shape=[jax.ShapeDtypeStruct(v.shape, v.dtype) for v in made],
+        in_specs=[vmem] * 4,
+        out_specs=[any_] * 4,
+        scratch_shapes=[pltpu.SemaphoreType.DMA((16,))],
+        compiler_params=pltpu.CompilerParams(vmem_limit_bytes=1024 * 1024),
+    )(*made)
+    return layer_out, table_grad[None], sum_in, sum_out
 
 
 def solution(mesh):

time: 80.6 us -> 66.5 us (0.83)
  Pallas kernels: 71.3 us -> 65.8 us
  other arithmetic: 5.4 us -> 0 us
  local copies, waits for them, and re-layouts: 3.05 us -> 0 us
    pallas_call x1, Pallas kernels: 71.3 us -> 62.9 us  [body(): pl.pallas_call(functools.partial(kernel, n, nz, count, cap, rows, tokens,...]
    mul x2 -> x0, other arithmetic: 5.4 us -> none  [the longest x1 4.29 us: body(): sum_in.astype(F32) * grad_scale]
    unnamed x9 -> x0, local copies, waits for them, and re-layouts: 3.05 us -> none
    pallas_call x0 -> x1, Pallas kernels: none -> 2.87 us  [body(): pl.pallas_call(store, out_shape=[jax.ShapeDtypeStruct(v.shape, v.dtype) f...]
where the time goes in v2:
time: 66.5 us; the launch traced here: 66.4 us
  Pallas kernels  65.8 us (99%)
    pallas_call x1, Pallas kernels, body(): pl.pallas_call(functools.partial(kernel, n, nz, count, cap, rows, tokens,...  62.9 us
    pallas_call x1, Pallas kernels, body(): pl.pallas_call(store, out_shape=[jax.ShapeDtypeStruct(v.shape, v.dtype) f...  2.87 us

profile of v2, /device:TPU:1, one launch (start us, length us, event | category | flops | bytes accessed | tf_op | source)
XLA Modules:
  0.0 66.4 jit_solution(15457189024095856187)
XLA Ops:
  0.6 62.9 %shard_map.102 = (bf16[256,512]{1,0:T(8,128)(2,1)S(1)}, bf16[1024,512]{1,0:T(8,128)(2,1)S(1)}, f32[512,2048]{1,0:T(8,128)S(1)}, f32[512,512]{1,0:T(8,128)S(1)}) custom-call(s32[8,32]{1,0:T(8,128)} %bitcast.5, s32[1,256]{1,0:T(1,128)} %bitcast.6, s32[1,8]{1,0:T(1,128)} %len_hbm.1, bf16[1024,512]{1,0:T(8,128)(2,1)} %table_hbm.1, bf16[512,2048]{1,0:T(8,128)(2,1)} %win_hbm.1, ...), custom_call_target="tpu_custom_call" | custom-call | tf_op jit(solution)/shard_map/pallas_call | solution.py:492
  63.5 2.9 %shard_map.103 = (bf16[256,512]{1,0:T(8,128)(2,1)}, bf16[1024,512]{1,0:T(8,128)(2,1)}, f32[512,2048]{1,0:T(8,128)}, f32[512,512]{1,0:T(8,128)}) custom-call(bf16[256,512]{1,0:T(8,128)(2,1)S(1)} %get-tuple-element.12.refs_0_, bf16[1024,512]{1,0:T(8,128)(2,1)S(1)} %get-tuple-element.13.refs_1_, f32[512,2048]{1,0:T(8,128)S(1)} %get-tuple-element.14.refs_2_, ...), custom_call_target="tpu_custom_call" | custom-call | tf_op jit(solution)/shard_map/pallas_call | solution.py:532

commit v3 on v2

--- a/solution.py
+++ b/solution.py
@@ -33,7 +33,7 @@
     out_ref, tg_ref, gin_ref, gout_ref,
     fetch_ref, slot_ref, len_ref, table_v, win_v, wout_v, cot_v,
     req_s, req_r, found, rows_r, sg_s, sg_r,
-    row_hot, emb, n32, normed, proj, dsil, dpre, weights, dfac, mixed, allowed,
+    row_hot, tok_hot, dg, gated_v, emb, n32, normed, proj, dsil, dpre, weights, dfac, mixed, allowed,
     g, pr, h, r1, s1, r2, s2, r3, a2,
     ro1, ro2, so2, ro3, full_ref, fullo_ref,
     load_sem, send_sem, recv_sem,
@@ -79,14 +79,14 @@
             )
         )
     ]
-    for copy in loads:
-        copy.start()
-
+    loads[0].start()
     barrier = pltpu.get_barrier_semaphore()
     for peer in ahead:
         pl.semaphore_signal(barrier, inc=1, device_id=(peer, z), device_id_type=MESH)
     for peer in zs:
         pl.semaphore_signal(barrier, inc=1, device_id=(t, peer), device_id_type=MESH)
+    for copy in loads[1:]:
+        copy.start()
 
     names = {}
     pending = []
@@ -129,7 +129,7 @@
     first = jnp.zeros((tokens, tokens), jnp.int32)
     for e in ends:
         first = jnp.where(pos_i >= e, e, first)
-    allowed[...] = jnp.where((pos_j >= first) & (pos_j <= pos_i), 1.0, 0.0).astype(F32)
+    allowed[...] = jnp.where((pos_j >= first) & (pos_j <= pos_i), 1.0, 0.0).astype(BF)
     slot_hot = jnp.where(
         lax.broadcasted_iota(jnp.int32, (slots, tokens), 0) == slot_ref[...], 1.0, 0.0
     ).astype(BF)
@@ -165,11 +165,14 @@
         for k in range(start, start + got):
             send(found.at[k], rows_r.at[t], (behind[k], z), "rows")
     rows_r[t] = found[count - 1]
+    tok_hot[...] = slot_hot.T
     for i in (4, 5, 6):
         loads[i].wait()
+    cot = cot_v[...]
+    dg[...] = mm(cot, wout_v[...], NT).astype(BF).astype(F32)
     arrived(rows_r.at[pl.ds(0, count - 1)], "rows")
 
-    e32 = mm(slot_hot, unpacked(rows_r), TN)
+    e32 = mm(tok_hot[...], unpacked(rows_r))
     emb[...] = e32
     cen = e32 - jnp.mean(e32, axis=1, keepdims=True)
     inv_e = lax.rsqrt(jnp.mean(cen * cen, axis=1, keepdims=True) + EPS)
@@ -182,8 +185,9 @@
     for b in range(4):
         p = mm(normed[...], win_v[:, cols(b)])
         sg = 0.5 + 0.5 * jnp.tanh(0.5 * p)
-        proj[:, cols(b)] = (p * sg).astype(BF)
-        dsil[:, cols(b)] = sg * (1.0 + p * (1.0 - sg))
+        act = p * sg
+        proj[:, cols(b)] = act.astype(BF)
+        dsil[:, cols(b)] = (sg + act * (1.0 - sg)).astype(BF)
 
     lanes = lax.broadcasted_iota(jnp.int32, (1, 128), 1)
     side = [
@@ -195,16 +199,28 @@
         return proj[:, b * width + 128 * i : b * width + 128 * (i + 1)]
 
     scale = (width // HEADS) ** -0.5
+    mid = tokens // 2
+
+    def lower(f, *arrays):
+        top = f(*(v[:mid, :mid] for v in arrays))
+        low = f(*(v[mid:] for v in arrays))
+        none = jnp.zeros((mid, tokens - mid), BF)
+        return [
+            jnp.concatenate([jnp.concatenate([a, none], axis=1), b], axis=0) for a, b in zip(top, low)
+        ]
+
+    def score(s, keep):
+        sg = 0.5 + 0.5 * jnp.tanh((0.5 * scale) * s)
+        act = (scale * s) * sg
+        return act.astype(BF) * keep, (sg + act * (1.0 - sg)).astype(BF) * (keep * BF(scale))
+
     for i in range(HEADS // 2):
         q, k, v = pair(2, i), pair(3, i), pair(1, i)
         part = None
         for j in range(2):
-            s = mm(q, k * side[j], NT) * scale
-            sg = 0.5 + 0.5 * jnp.tanh(0.5 * s)
-            keep = allowed[...]
-            w = (keep * (s * sg)).astype(BF)
+            w, factor = lower(score, mm(q, k * side[j], NT), allowed[...])
             weights[2 * i + j] = w
-            dfac[2 * i + j] = (keep * scale) * (sg * (1.0 + s * (1.0 - sg)))
+            dfac[2 * i + j] = factor
             term = mm(w, v * side[j])
             part = term if part is None else part + term
         mixed[:, 128 * i : 128 * (i + 1)] = part
@@ -215,8 +231,7 @@
     nm = cen * inv_m
     u32 = proj[:, cols(0)].astype(F32)
     gated = (nm * u32).astype(BF)
-    cot = cot_v[...]
-    out_ref[...] = (emb[...] + mm(gated, wout_v[...])).astype(BF)
+    gated_v[...] = gated
 
     own = rows_of(c * R0, R0)
     other = rows_of((1 - c) * R0, R0)
@@ -227,34 +242,35 @@
     def first_peers(b):
         return (xs, x, ys, y) if b % 2 == 0 else (ys, y, xs, x)
 
-    def plane(v, peers):
+    def plane(v):
         return [plus(v, d, n) for d in steps]
 
     def pair_sum(b):
         arrived(pr.at[b], f"pair{b}")
         h[b] = (g[b, own].astype(F32) + pr[b].astype(F32)).astype(BF)
         if b < 4:
-            peers, v, _, _ = first_peers(b)
-            for k, (peer, place) in enumerate(zip(peers, plane(v, peers))):
-                send(h.at[b, rows_of(place * R1, R1)], r1.at[b, k], (peer, z), f"first{b}")
+            peers, v, _, w = first_peers(b)
+            for j, sub in enumerate(plane(w) + [w]):
+                for k, (peer, place) in enumerate(zip(peers, plane(v))):
+                    send(h.at[b, rows_of(place * R1 + sub * R2, R2)], r1.at[b, j, k], (peer, z), f"first{b}_{j}")
         else:
             for k, place in enumerate(zs):
                 send(h.at[b, rows_of(place * (R0 // nz), R0 // nz)], ro1.at[k], (t, place), "o_z")
 
     def first_sum(b):
-        arrived(r1.at[b], f"first{b}")
         _, v, peers, w = first_peers(b)
-        acc = h[b, rows_of(v * R1, R1)].astype(F32)
-        for k in range(n - 1):
-            acc = acc + r1[b, k].astype(F32)
-        s1[b] = acc.astype(BF)
-        for k, (peer, place) in enumerate(zip(peers, plane(w, peers))):
-            send(s1.at[b, rows_of(place * R2, R2)], r2.at[b, k], (peer, z), f"second{b}")
+        for j, sub in enumerate(plane(w) + [w]):
+            arrived(r1.at[b, j], f"first{b}_{j}")
+            acc = h[b, rows_of(v * R1 + sub * R2, R2)].astype(F32)
+            for k in range(n - 1):
+                acc = acc + r1[b, j, k].astype(F32)
+            s1[b, j] = acc.astype(BF)
+            if j < n - 1:
+                send(s1.at[b, j], r2.at[b, j], (peers[j], z), f"second{b}")
 
     def second_sum(b):
         arrived(r2.at[b], f"second{b}")
-        _, _, _, w = first_peers(b)
-        acc = s1[b, rows_of(w * R2, R2)].astype(F32)
+        acc = s1[b, n - 1].astype(F32)
         for k in range(n - 1):
             acc = acc + r2[b, k].astype(F32)
         s2[b // 2, :, cols(b % 2)] = acc.astype(BF)
@@ -281,16 +297,25 @@
             _, v, peers, w = first_peers(b)
             mine = rows_of(c * R0 + v * R1 + w * R2, R2)
             full_ref[mine, cols(b)] = a2[i, :, cols(b % 2)]
-            for peer in peers:
-                strip = full_ref.at[mine, cols(b)]
-                send(strip, strip, (peer, z), f"g_second{b}")
-
-    def back_second(b):
-        arrived(r2.at[b], f"g_second{b}")
-        peers, v, _, _ = first_peers(b)
-        strip = full_ref.at[rows_of(c * R0 + v * R1, R1), cols(b)]
-        for k, peer in enumerate(peers):
-            send(strip, strip, (peer, z), f"g_first{b}_{k}")
+            strip = full_ref.at[mine, cols(b)]
+            for k, peer in enumerate(peers):
+                send(strip, strip, (peer, z), f"g_second{b}_{k}")
+        for b in (2 * i, 2 * i + 1):
+            pass_on(b, n - 1)
+
+    def pass_on(b, k):
+        peers, v, _, w = first_peers(b)
+        place = plus(w, n - steps[k], n) if k < n - 1 else w
+        strip = full_ref.at[rows_of(c * R0 + v * R1 + place * R2, R2), cols(b)]
+        for i, peer in enumerate(peers):
+            send(strip, strip, (peer, z), f"g_first{b}_{i}")
+
+    def back_second(b, k):
+        arrived(s1.at[b, 0], f"g_second{b}_{k}")
+        pass_on(b, k)
+
+    def own_strip(b):
+        strip = full_ref.at[strip_of(c, b, n - 1), cols(b)]
         send(strip, strip, (partner, z), f"g_pair{b}_{n - 1}")
 
     def strip_of(core, b, k):
@@ -311,19 +336,18 @@
         arrived(s1.at[b], f"g_pair{b}_{k}")
         finish(1 - c, b, k)
 
-    d_gated = mm(cot, wout_v[...], NT).astype(BF).astype(F32)
+    d_gated = dg[...]
     g[4] = mm(gated, cot, TN).astype(BF)
     to_partner(4)
     normed_t = normed[...].T
 
     def weight_grad(b, d_proj):
-        d = (d_proj.astype(BF).astype(F32) * dsil[:, cols(b)]).astype(BF)
+        d = d_proj.astype(BF) * dsil[:, cols(b)]
         dpre[:, cols(b)] = d
         g[b] = mm(normed_t, d).astype(BF)
         to_partner(b)
 
     weight_grad(0, d_gated * nm)
-    pair_sum(4)
 
     gn = d_gated * u32
     dm = inv_m * (
@@ -338,8 +362,8 @@
             term = mm(weights[2 * i + j], dm_i * side[j], TN)
             part = term if part is None else part + term
         d_v.append(part)
+    pair_sum(4)
     weight_grad(1, jnp.concatenate(d_v, axis=1))
-    pair_sum(0)
 
     d_q, d_k = [], []
     for i in range(HEADS // 2):
@@ -347,8 +371,9 @@
         dm_i = mixed[:, 128 * i : 128 * (i + 1)].astype(BF)
         part_q = part_k = None
         for j in range(2):
-            dw = mm(dm_i, v * side[j], NT).astype(BF).astype(F32)
-            ds = (dw * dfac[2 * i + j]).astype(BF)
+            (ds,) = lower(
+                lambda dw, factor: (dw.astype(BF) * factor,), mm(dm_i, v * side[j], NT), dfac[2 * i + j]
+            )
             term_q = mm(ds, k * side[j])
             term_k = mm(ds, q * side[j], TN)
             part_q = term_q if part_q is None else part_q + term_q
@@ -356,12 +381,15 @@
         d_q.append(part_q)
         d_k.append(part_k)
         if i == 0:
+            pair_sum(0)
+        if i == 2:
             pair_sum(1)
     weight_grad(2, jnp.concatenate(d_q, axis=1))
     weight_grad(3, jnp.concatenate(d_k, axis=1))
     pair_sum(2)
     pair_sum(3)
 
+    out_ref[...] = (emb[...] + mm(gated_v[...], wout_v[...])).astype(BF)
     dn = mm(dpre[...], win_v[...], NT).astype(BF).astype(F32)
     first_sum(0)
     first_sum(1)
@@ -380,7 +408,7 @@
     for k in range(nz - 1):
         acc = acc + ro1[k].astype(F32)
     h[4, rows_of(z * RZ, RZ)] = acc.astype(BF)
-    for k, (peer, place) in enumerate(zip(xs, plane(x, xs))):
+    for k, (peer, place) in enumerate(zip(xs, plane(x))):
         send(
             h.at[4, rows_of(z * RZ, RZ), rows_of(place * CX, CX)], ro2.at[k], (peer, z), "o_x"
         )
@@ -419,13 +447,15 @@
         strip = fullo_ref.at[orows]
         send(strip, strip, (t, peer), "o_gz")
     back_z(0)
+    back_z(1)
     arrived(sg_r.at[pl.ds(0, count - 1)], "slot")
     tg_ref[...] = mm(row_hot[...], unpacked(sg_r), TN).astype(BF)
-    back_z(1)
-    back_second(0)
-    back_second(1)
-    back_second(2)
-    back_second(3)
+    for i in (0, 2):
+        for k in reversed(range(n - 1)):
+            back_second(i, k)
+            back_second(i + 1, k)
+        own_strip(i)
+        own_strip(i + 1)
     for b in range(4):
         finish(c, b, n - 1)
     for k in reversed(range(n - 1)):
@@ -502,20 +532,20 @@
             V((count, 1, 128), jnp.int32), V((count, 1, 128), jnp.int32),
             V((count, 2 * cap, half), BF), V((count, 2 * cap, half), BF),
             V((count, 2 * cap, half), BF), V((count, 2 * cap, half), BF),
-            V((slots, rows), BF), V((tokens, width), F32), V((tokens, width), F32), V((tokens, width), BF),
-            V((tokens, 4 * width), BF), V((tokens, 4 * width), F32), V((tokens, 4 * width), BF),
-            V((HEADS, tokens, tokens), BF), V((HEADS, tokens, tokens), F32),
-            V((tokens, width), F32), V((tokens, tokens), F32),
+            V((slots, rows), BF), V((tokens, slots), BF), V((tokens, width), F32), V((tokens, width), BF), V((tokens, width), F32), V((tokens, width), F32), V((tokens, width), BF),
+            V((tokens, 4 * width), BF), V((tokens, 4 * width), BF), V((tokens, 4 * width), BF),
+            V((HEADS, tokens, tokens), BF), V((HEADS, tokens, tokens), BF),
+            V((tokens, width), F32), V((tokens, tokens), BF),
             V((5, width, width), BF), V((5, R0, width), BF), V((5, R0, width), BF),
-            V((4, n - 1, R1, width), BF), V((4, R1, width), BF),
+            V((4, n, n - 1, R2, width), BF), V((4, n, R2, width), BF),
             V((4, n - 1, R2, width), BF), V((2, R2, 2 * width), BF),
             V((2, nz - 1, R2, CZ), BF), V((2, R2, 2 * width), BF),
             V((nz - 1, R0 // nz, width), BF), V((n - 1, R0 // nz, width // n), BF),
             V((R0 // nz, width // n), BF), V((n, R0 // nz, width // n), BF),
             V((width, 4 * width), BF), V((width, width), BF),
             pltpu.SemaphoreType.DMA((7,)),
-            pltpu.SemaphoreType.DMA((64,)),
-            pltpu.SemaphoreType.DMA((64,)),
+            pltpu.SemaphoreType.DMA((96,)),
+            pltpu.SemaphoreType.DMA((96,)),
         ],
         compiler_params=pltpu.CompilerParams(
             collective_id=0, has_side_effects=True, vmem_limit_bytes=40 * 1024 * 1024

time: 66.5 us -> 65.1 us (0.979)
  Pallas kernels: 65.8 us -> 64.4 us
    pallas_call x1, Pallas kernels: 62.9 us -> 61.5 us  [body(): pl.pallas_call(functools.partial(kernel, n, nz, count, cap, rows, tokens,...]
where the time goes in v3:
time: 65.1 us; the launch traced here: 65 us
  Pallas kernels  64.4 us (99%)
    pallas_call x1, Pallas kernels, body(): pl.pallas_call(functools.partial(kernel, n, nz, count, cap, rows, tokens,...  61.5 us
    pallas_call x1, Pallas kernels, body(): pl.pallas_call(store, out_shape=[jax.ShapeDtypeStruct(v.shape, v.dtype) f...  2.87 us

profile of v3, /device:TPU:1, one launch (start us, length us, event | category | flops | bytes accessed | tf_op | source)
XLA Modules:
  0.0 65.0 jit_solution(6589376828453117156)
XLA Ops:
  0.6 61.5 %shard_map.102 = (bf16[256,512]{1,0:T(8,128)(2,1)S(1)}, bf16[1024,512]{1,0:T(8,128)(2,1)S(1)}, f32[512,2048]{1,0:T(8,128)S(1)}, f32[512,512]{1,0:T(8,128)S(1)}) custom-call(s32[8,32]{1,0:T(8,128)} %bitcast.5, s32[1,256]{1,0:T(1,128)} %bitcast.6, s32[1,8]{1,0:T(1,128)} %len_hbm.1, bf16[1024,512]{1,0:T(8,128)(2,1)} %table_hbm.1, bf16[512,2048]{1,0:T(8,128)(2,1)} %win_hbm.1, ...), custom_call_target="tpu_custom_call" | custom-call | tf_op jit(solution)/shard_map/pallas_call | solution.py:522
  62.1 2.9 %shard_map.103 = (bf16[256,512]{1,0:T(8,128)(2,1)}, bf16[1024,512]{1,0:T(8,128)(2,1)}, f32[512,2048]{1,0:T(8,128)}, f32[512,512]{1,0:T(8,128)}) custom-call(bf16[256,512]{1,0:T(8,128)(2,1)S(1)} %get-tuple-element.12.refs_0_, bf16[1024,512]{1,0:T(8,128)(2,1)S(1)} %get-tuple-element.13.refs_1_, f32[512,2048]{1,0:T(8,128)S(1)} %get-tuple-element.14.refs_2_, ...), custom_call_target="tpu_custom_call" | custom-call | tf_op jit(solution)/shard_map/pallas_call | solution.py:562

commit v4 on v3

--- a/solution.py
+++ b/solution.py
@@ -273,31 +273,29 @@
         acc = s1[b, n - 1].astype(F32)
         for k in range(n - 1):
             acc = acc + r2[b, k].astype(F32)
-        s2[b // 2, :, cols(b % 2)] = acc.astype(BF)
+        for i in range(width // CZ):
+            s2[b // 2, b % 2 * (width // CZ) + i] = acc[:, i * CZ : (i + 1) * CZ].astype(BF)
         if b % 2 == 1:
             for k, place in enumerate(zs):
-                send(
-                    s2.at[b // 2, :, rows_of(place * CZ, CZ)], r3.at[b // 2, k], (t, place), f"last{b // 2}"
-                )
-
-    zcols = rows_of(z * CZ, CZ)
+                send(s2.at[b // 2, place], r3.at[b // 2, k], (t, place), f"last{b // 2}")
 
     def last_sum(i):
         arrived(r3.at[i], f"last{i}")
-        acc = s2[i, :, zcols].astype(F32)
+        acc = s2[i, z].astype(F32)
         for k in range(nz - 1):
             acc = acc + r3[i, k].astype(F32)
-        a2[i, :, zcols] = acc.astype(BF)
+        a2[i, z] = acc.astype(BF)
         for peer in zs:
-            send(a2.at[i, :, zcols], a2.at[i, :, zcols], (t, peer), f"g_z{i}")
+            send(a2.at[i, z], a2.at[i, z], (t, peer), f"g_z{i}")
 
     def back_z(i):
-        arrived(a2.at[i, :, pl.ds(0, CZ * (nz - 1))], f"g_z{i}")
+        arrived(a2.at[i, pl.ds(0, nz - 1)], f"g_z{i}")
         for b in (2 * i, 2 * i + 1):
             _, v, peers, w = first_peers(b)
             mine = rows_of(c * R0 + v * R1 + w * R2, R2)
-            full_ref[mine, cols(b)] = a2[i, :, cols(b % 2)]
-            strip = full_ref.at[mine, cols(b)]
+            for j in range(width // CZ):
+                full_ref[b, mine, j * CZ : (j + 1) * CZ] = a2[i, b % 2 * (width // CZ) + j]
+            strip = full_ref.at[b, mine]
             for k, peer in enumerate(peers):
                 send(strip, strip, (peer, z), f"g_second{b}_{k}")
         for b in (2 * i, 2 * i + 1):
@@ -306,7 +304,7 @@
     def pass_on(b, k):
         peers, v, _, w = first_peers(b)
         place = plus(w, n - steps[k], n) if k < n - 1 else w
-        strip = full_ref.at[rows_of(c * R0 + v * R1 + place * R2, R2), cols(b)]
+        strip = full_ref.at[b, rows_of(c * R0 + v * R1 + place * R2, R2)]
         for i, peer in enumerate(peers):
             send(strip, strip, (peer, z), f"g_first{b}_{i}")
 
@@ -315,7 +313,7 @@
         pass_on(b, k)
 
     def own_strip(b):
-        strip = full_ref.at[strip_of(c, b, n - 1), cols(b)]
+        strip = full_ref.at[b, strip_of(c, b, n - 1)]
         send(strip, strip, (partner, z), f"g_pair{b}_{n - 1}")
 
     def strip_of(core, b, k):
@@ -325,11 +323,11 @@
 
     def finish(core, b, k):
         strip = strip_of(core, b, k)
-        gin_ref[strip, cols(b)] = full_ref[strip, cols(b)].astype(F32) * grad_scale
+        gin_ref[strip, cols(b)] = full_ref[b, strip].astype(F32) * grad_scale
 
     def back_first(b, k):
         arrived(s1.at[b], f"g_first{b}_{k}")
-        strip = full_ref.at[strip_of(c, b, k), cols(b)]
+        strip = full_ref.at[b, strip_of(c, b, k)]
         send(strip, strip, (partner, z), f"g_pair{b}_{k}")
 
     def back_pair(b, k):
@@ -391,8 +389,6 @@
 
     out_ref[...] = (emb[...] + mm(gated_v[...], wout_v[...])).astype(BF)
     dn = mm(dpre[...], win_v[...], NT).astype(BF).astype(F32)
-    first_sum(0)
-    first_sum(1)
     nv = n32[...]
     de = cot.astype(F32) + inv_e * (
         dn - jnp.mean(dn, axis=1, keepdims=True) - nv * jnp.mean(dn * nv, axis=1, keepdims=True)
@@ -403,51 +399,63 @@
 
     RZ = R0 // nz
     CX = width // n
-    arrived(ro1, "o_z")
-    acc = h[4, rows_of(z * RZ, RZ)].astype(F32)
-    for k in range(nz - 1):
-        acc = acc + ro1[k].astype(F32)
-    h[4, rows_of(z * RZ, RZ)] = acc.astype(BF)
-    for k, (peer, place) in enumerate(zip(xs, plane(x))):
-        send(
-            h.at[4, rows_of(z * RZ, RZ), rows_of(place * CX, CX)], ro2.at[k], (peer, z), "o_x"
-        )
-    second_sum(0)
-    second_sum(1)
-    first_sum(2)
-    first_sum(3)
-    arrived(ro2, "o_x")
-    acc = h[4, rows_of(z * RZ, RZ), rows_of(x * CX, CX)].astype(F32)
-    for k in range(n - 1):
-        acc = acc + ro2[k].astype(F32)
-    so2[...] = acc.astype(BF)
-    ro3[y] = so2[...]
-    for peer in ys:
-        send(so2, ro3.at[y], (peer, z), "o_y")
-    second_sum(2)
-    second_sum(3)
-    for k, peer in enumerate(ahead):
-        send(sg_s.at[peer], sg_r.at[k], (peer, z), "slot")
-    last_sum(0)
-
-    arrived(ro3.at[pl.ds(0, n - 1)], "o_y")
-    acc = ro3[0].astype(F32)
-    for k in range(1, n):
-        acc = acc + ro3[k].astype(F32)
     orows = rows_of(c * R0 + z * RZ, RZ)
     ocols = rows_of(x * CX, CX)
-    fullo_ref[orows, ocols] = acc.astype(BF)
-    for peer in xs:
-        strip = fullo_ref.at[orows, ocols]
-        send(strip, strip, (peer, z), "o_gx")
-
+
+    def out_z():
+        arrived(ro1, "o_z")
+        acc = h[4, rows_of(z * RZ, RZ)].astype(F32)
+        for k in range(nz - 1):
+            acc = acc + ro1[k].astype(F32)
+        h[4, rows_of(z * RZ, RZ)] = acc.astype(BF)
+        for k, (peer, place) in enumerate(zip(xs, plane(x))):
+            send(
+                h.at[4, rows_of(z * RZ, RZ), rows_of(place * CX, CX)], ro2.at[k], (peer, z), "o_x"
+            )
+
+    def out_x():
+        arrived(ro2, "o_x")
+        acc = h[4, rows_of(z * RZ, RZ), ocols].astype(F32)
+        for k in range(n - 1):
+            acc = acc + ro2[k].astype(F32)
+        so2[...] = acc.astype(BF)
+        ro3[y] = so2[...]
+        for peer in ys:
+            send(so2, ro3.at[y], (peer, z), "o_y")
+
+    def out_y():
+        arrived(ro3.at[pl.ds(0, n - 1)], "o_y")
+        acc = ro3[0].astype(F32)
+        for k in range(1, n):
+            acc = acc + ro3[k].astype(F32)
+        fullo_ref[orows, ocols] = acc.astype(BF)
+        for peer in xs:
+            strip = fullo_ref.at[orows, ocols]
+            send(strip, strip, (peer, z), "o_gx")
+
+    def out_back_x():
+        arrived(ro2, "o_gx")
+        for peer in zs:
+            strip = fullo_ref.at[orows]
+            send(strip, strip, (t, peer), "o_gz")
+
+    def slots_out():
+        for k, peer in enumerate(ahead):
+            send(sg_s.at[peer], sg_r.at[k], (peer, z), "slot")
+
+    for b in range(4):
+        first_sum(b)
+    for b in range(4):
+        second_sum(b)
+    out_z()
+    slots_out()
+    last_sum(0)
+    out_x()
     last_sum(1)
-    arrived(ro2, "o_gx")
-    for peer in zs:
-        strip = fullo_ref.at[orows]
-        send(strip, strip, (t, peer), "o_gz")
+    out_y()
     back_z(0)
     back_z(1)
+    out_back_x()
     arrived(sg_r.at[pl.ds(0, count - 1)], "slot")
     tg_ref[...] = mm(row_hot[...], unpacked(sg_r), TN).astype(BF)
     for i in (0, 2):
@@ -538,11 +546,11 @@
             V((tokens, width), F32), V((tokens, tokens), BF),
             V((5, width, width), BF), V((5, R0, width), BF), V((5, R0, width), BF),
             V((4, n, n - 1, R2, width), BF), V((4, n, R2, width), BF),
-            V((4, n - 1, R2, width), BF), V((2, R2, 2 * width), BF),
-            V((2, nz - 1, R2, CZ), BF), V((2, R2, 2 * width), BF),
+            V((4, n - 1, R2, width), BF), V((2, nz, R2, CZ), BF),
+            V((2, nz - 1, R2, CZ), BF), V((2, nz, R2, CZ), BF),
             V((nz - 1, R0 // nz, width), BF), V((n - 1, R0 // nz, width // n), BF),
             V((R0 // nz, width // n), BF), V((n, R0 // nz, width // n), BF),
-            V((width, 4 * width), BF), V((width, width), BF),
+            V((4, width, width), BF), V((width, width), BF),
             pltpu.SemaphoreType.DMA((7,)),
             pltpu.SemaphoreType.DMA((96,)),
             pltpu.SemaphoreType.DMA((96,)),

time: 65.1 us -> 63.6 us (0.977)
  Pallas kernels: 64.4 us -> 62.8 us
    pallas_call x1, Pallas kernels: 61.5 us -> 59.9 us  [body(): pl.pallas_call(functools.partial(kernel, n, nz, count, cap, rows, tokens,...]
where the time goes in v4:
time: 63.6 us; the launch traced here: 63.5 us
  Pallas kernels  62.8 us (99%)
  between operations  0.64 us (1%)
    pallas_call x1, Pallas kernels, body(): pl.pallas_call(functools.partial(kernel, n, nz, count, cap, rows, tokens,...  59.9 us
    pallas_call x1, Pallas kernels, body(): pl.pallas_call(store, out_shape=[jax.ShapeDtypeStruct(v.shape, v.dtype) f...  2.87 us

profile of v4, /device:TPU:1, one launch (start us, length us, event | category | flops | bytes accessed | tf_op | source)
XLA Modules:
  0.0 63.5 jit_solution(16204971402847755760)
XLA Ops:
  0.6 59.9 %shard_map.102 = (bf16[256,512]{1,0:T(8,128)(2,1)S(1)}, bf16[1024,512]{1,0:T(8,128)(2,1)S(1)}, f32[512,2048]{1,0:T(8,128)S(1)}, f32[512,512]{1,0:T(8,128)S(1)}) custom-call(s32[8,32]{1,0:T(8,128)} %bitcast.5, s32[1,256]{1,0:T(1,128)} %bitcast.6, s32[1,8]{1,0:T(1,128)} %len_hbm.1, bf16[1024,512]{1,0:T(8,128)(2,1)} %table_hbm.1, bf16[512,2048]{1,0:T(8,128)(2,1)} %win_hbm.1, ...), custom_call_target="tpu_custom_call" | custom-call | tf_op jit(solution)/shard_map/pallas_call | solution.py:530
  60.6 2.9 %shard_map.103 = (bf16[256,512]{1,0:T(8,128)(2,1)}, bf16[1024,512]{1,0:T(8,128)(2,1)}, f32[512,2048]{1,0:T(8,128)}, f32[512,512]{1,0:T(8,128)}) custom-call(bf16[256,512]{1,0:T(8,128)(2,1)S(1)} %get-tuple-element.12.refs_0_, bf16[1024,512]{1,0:T(8,128)(2,1)S(1)} %get-tuple-element.13.refs_1_, f32[512,2048]{1,0:T(8,128)S(1)} %get-tuple-element.14.refs_2_, ...), custom_call_target="tpu_custom_call" | custom-call | tf_op jit(solution)/shard_map/pallas_call | solution.py:570

commit v5 on v4

--- a/solution.py
+++ b/solution.py
@@ -456,14 +456,15 @@
     back_z(0)
     back_z(1)
     out_back_x()
-    arrived(sg_r.at[pl.ds(0, count - 1)], "slot")
-    tg_ref[...] = mm(row_hot[...], unpacked(sg_r), TN).astype(BF)
     for i in (0, 2):
         for k in reversed(range(n - 1)):
             back_second(i, k)
             back_second(i + 1, k)
         own_strip(i)
         own_strip(i + 1)
+        if i == 0:
+            arrived(sg_r.at[pl.ds(0, count - 1)], "slot")
+            tg_ref[...] = mm(row_hot[...], unpacked(sg_r), TN).astype(BF)
     for b in range(4):
         finish(c, b, n - 1)
     for k in reversed(range(n - 1)):

time: 63.6 us -> 63.6 us (level)
  no operation moved by 1% of the time
where the time goes in v5:
time: 63.6 us; the launch traced here: 63.5 us
  Pallas kernels  62.8 us (99%)
  between operations  0.64 us (1%)
    pallas_call x1, Pallas kernels, body(): pl.pallas_call(functools.partial(kernel, n, nz, count, cap, rows, tokens,...  59.9 us
    pallas_call x1, Pallas kernels, body(): pl.pallas_call(store, out_shape=[jax.ShapeDtypeStruct(v.shape, v.dtype) f...  2.87 us

profile of v5, /device:TPU:1, one launch (start us, length us, event | category | flops | bytes accessed | tf_op | source)
XLA Modules:
  0.0 63.5 jit_solution(16831288371047788218)
XLA Ops:
  0.6 59.9 %shard_map.102 = (bf16[256,512]{1,0:T(8,128)(2,1)S(1)}, bf16[1024,512]{1,0:T(8,128)(2,1)S(1)}, f32[512,2048]{1,0:T(8,128)S(1)}, f32[512,512]{1,0:T(8,128)S(1)}) custom-call(s32[8,32]{1,0:T(8,128)} %bitcast.5, s32[1,256]{1,0:T(1,128)} %bitcast.6, s32[1,8]{1,0:T(1,128)} %len_hbm.1, bf16[1024,512]{1,0:T(8,128)(2,1)} %table_hbm.1, bf16[512,2048]{1,0:T(8,128)(2,1)} %win_hbm.1, ...), custom_call_target="tpu_custom_call" | custom-call | tf_op jit(solution)/shard_map/pallas_call | solution.py:531
  60.6 2.9 %shard_map.103 = (bf16[256,512]{1,0:T(8,128)(2,1)}, bf16[1024,512]{1,0:T(8,128)(2,1)}, f32[512,2048]{1,0:T(8,128)}, f32[512,512]{1,0:T(8,128)}) custom-call(bf16[256,512]{1,0:T(8,128)(2,1)S(1)} %get-tuple-element.12.refs_0_, bf16[1024,512]{1,0:T(8,128)(2,1)S(1)} %get-tuple-element.13.refs_1_, f32[512,2048]{1,0:T(8,128)S(1)} %get-tuple-element.14.refs_2_, ...), custom_call_target="tpu_custom_call" | custom-call | tf_op jit(solution)/shard_map/pallas_call | solution.py:571

commit v6 on v4

--- a/solution.py
+++ b/solution.py
@@ -380,7 +380,7 @@
         d_k.append(part_k)
         if i == 0:
             pair_sum(0)
-        if i == 2:
+        if i == 1:
             pair_sum(1)
     weight_grad(2, jnp.concatenate(d_q, axis=1))
     weight_grad(3, jnp.concatenate(d_k, axis=1))

time: 63.6 us -> 63.7 us (level)
  no operation moved by 1% of the time
where the time goes in v6:
time: 63.7 us; the launch traced here: 63.5 us
  Pallas kernels  62.9 us (99%)
  between operations  0.64 us (1%)
    pallas_call x1, Pallas kernels, body(): pl.pallas_call(functools.partial(kernel, n, nz, count, cap, rows, tokens,...  60 us
    pallas_call x1, Pallas kernels, body(): pl.pallas_call(store, out_shape=[jax.ShapeDtypeStruct(v.shape, v.dtype) f...  2.87 us

profile of v6, /device:TPU:1, one launch (start us, length us, event | category | flops | bytes accessed | tf_op | source)
XLA Modules:
  0.0 63.5 jit_solution(10092632448044530223)
XLA Ops:
  0.6 60.0 %shard_map.102 = (bf16[256,512]{1,0:T(8,128)(2,1)S(1)}, bf16[1024,512]{1,0:T(8,128)(2,1)S(1)}, f32[512,2048]{1,0:T(8,128)S(1)}, f32[512,512]{1,0:T(8,128)S(1)}) custom-call(s32[8,32]{1,0:T(8,128)} %bitcast.5, s32[1,256]{1,0:T(1,128)} %bitcast.6, s32[1,8]{1,0:T(1,128)} %len_hbm.1, bf16[1024,512]{1,0:T(8,128)(2,1)} %table_hbm.1, bf16[512,2048]{1,0:T(8,128)(2,1)} %win_hbm.1, ...), custom_call_target="tpu_custom_call" | custom-call | tf_op jit(solution)/shard_map/pallas_call | solution.py:530
  60.7 2.9 %shard_map.103 = (bf16[256,512]{1,0:T(8,128)(2,1)}, bf16[1024,512]{1,0:T(8,128)(2,1)}, f32[512,2048]{1,0:T(8,128)}, f32[512,512]{1,0:T(8,128)}) custom-call(bf16[256,512]{1,0:T(8,128)(2,1)S(1)} %get-tuple-element.12.refs_0_, bf16[1024,512]{1,0:T(8,128)(2,1)S(1)} %get-tuple-element.13.refs_1_, f32[512,2048]{1,0:T(8,128)S(1)} %get-tuple-element.14.refs_2_, ...), custom_call_target="tpu_custom_call" | custom-call | tf_op jit(solution)/shard_map/pallas_call | solution.py:570
